TPU v7x, 256 devices: a whole 4x4x8 slice. The times are simulated.
256 devices in a mesh: group: 2 (over core), tile: 128 (over z, x, y).
Axes of the slice: x: 4, y: 4, z: 8, core: 2. Of those that a mesh axis runs over, the one named last changes fastest.
Arguments:
- species_amounts: float32 [2, 220, 8, 16384], P('group', None, None, 'tile'), may hold values from 0.01 to 2
- air_warmth_kelvin: float32 [8, 16384], P(None, 'tile'), may hold values from 200 to 300
- sunlight_strength: float32 [8, 16384], P(None, 'tile'), may hold values from 0.1 to 1
- wind_stability_numbers: float32 [8, 16384], P(None, 'tile'), may hold values from -0.8 to 0.8
- illuminated_marker: int32 [16384], replicated, may hold values from 0 to 1, as said below
- position_vertical_lookup: int32 [16384], replicated, may hold values from 0 to 16383, as said below
- speed_constants: float32 [500], replicated, may hold values from 0.02 to 3
- barrier_kelvins: float32 [500], replicated, may hold values from 0 to 1200
- consumed_species: int32 [2, 500], replicated, may hold values from 0 to 219, as said below
- outcome_species: int32 [2, 500], replicated, may hold values from 0 to 219
- outcome_fractions: float32 [2, 500], replicated, may hold values from 0.3 to 1
Outputs:
- state: float32 [2, 220, 8, 16384], P('group', None, None, 'tile')
Inputs may be any that keep to these rules, and one draw needn't show every extreme that they name: `illuminated_marker`: 1 exactly on the columns of 64 consecutive tiles of 128 columns, counted cyclically along the slab from a random tile. `position_vertical_lookup`: A permutation of the columns; slot o * 128 + s + j, for j below 1, holds a column of tile s. `consumed_species`: the two reactants of a reaction differ; the second is not read for the first 64 reactions.
All inputs are finite; a program needn't handle non-finite values.
Results may differ from a plain program's by a relative error of at most 0.0003.
Values sent between devices are 32-bit elements; how exact they have to be, the bound alone decides.
No kernel may reach another device: no remote copies, remote signals or barrier semaphores. Data moves between devices by JAX's collectives and lax.ppermute only.
A program may use at most 64 MiB of HBM per device.

v0:
```python
import jax
import jax.numpy as jnp
from jax import lax
from jax.experimental import pallas as pl
from jax.experimental.pallas import tpu as pltpu
from jax.sharding import PartitionSpec as P

SPEC = 220
REAC = 500
PHOT = 64
LAYERS = 8
COLS = 128
ADV_STEPS = 4
ITER_NIGHT = 2
ITER_DAY = 4

HALF = LAYERS // 2
ROWS = SPEC * LAYERS
SPAD = 224
KDIM = 256
RPAD = 512
CELLS = HALF * COLS
CHUNK = 256
EDGE = 4
DARK = -1024.0

ORDER = [z * 16 + xy for z in (7, 3, 6, 2, 5, 1, 4, 0) for xy in range(15, -1, -1)]

VMEM = pl.BlockSpec(memory_space=pltpu.VMEM)
SMEM = pl.BlockSpec(memory_space=pltpu.SMEM)
ANY = pl.BlockSpec(memory_space=pl.ANY)
HBM = pl.BlockSpec(memory_space=pltpu.HBM)
PARAMS = pltpu.CompilerParams(vmem_limit_bytes=24 * 1024 * 1024)


def high_low(value):
    high = value.astype(jnp.bfloat16)
    return high, (value - high.astype(jnp.float32)).astype(jnp.bfloat16)


def dot(a, b):
    return jnp.dot(a, b, preferred_element_type=jnp.float32)


def tile_at(place):
    step = place // 16
    return (7 - step // 2 - 4 * (step % 2)) * 16 + 15 - place % 16


def place_of(tile):
    z = tile // 16
    return (2 * (3 - z % 4) + 1 - z // 4) * 16 + 15 - tile % 16


def prepare_kernel(
    tile_of,
    heat,
    light,
    consumed,
    outcome,
    fractions,
    speeds,
    barriers,
    weights,
    gather,
    terms,
    heat_here,
    light_here,
    consumed_here,
    outcome_here,
    fractions_here,
    speeds_here,
    barriers_here,
    turning,
    sems,
):
    group = tile_of[0]
    copies = [
        pltpu.make_async_copy(source, target, sems.at[place])
        for place, (source, target) in enumerate(
            (
                (consumed, consumed_here),
                (outcome, outcome_here),
                (fractions, fractions_here),
                (speeds, speeds_here),
                (barriers, barriers_here),
                (heat, heat_here),
                (light, light_here),
            )
        )
    ]
    for copy in copies:
        copy.start()
    spare = pl.ds(RPAD - COLS, COLS)
    weights[:, spare] = jnp.zeros((3 * SPAD, COLS), jnp.bfloat16)
    turning[:, spare] = jnp.zeros((KDIM, COLS), jnp.float32)
    for copy in copies:
        copy.wait()

    used = pl.ds(0, REAC)
    species = lax.broadcasted_iota(jnp.int32, (SPAD, REAC), 0)
    thermal = lax.broadcasted_iota(jnp.int32, (1, REAC), 1) >= PHOT
    second = jnp.where(thermal, consumed_here[1:2, :], -1)
    consuming = jnp.where(species == consumed_here[0:1, :], 1.0, 0.0) + jnp.where(
        species == second, 1.0, 0.0
    )
    producing = jnp.where(species == outcome_here[0:1, :], fractions_here[0:1, :], 0.0) + jnp.where(
        species == outcome_here[1:2, :], fractions_here[1:2, :], 0.0
    )
    producing_high, producing_low = high_low(producing)
    weights[pl.ds(0, SPAD), used] = consuming.astype(jnp.bfloat16)
    weights[pl.ds(SPAD, SPAD), used] = producing_high
    weights[pl.ds(2 * SPAD, SPAD), used] = producing_low

    speed = lax.log2(speeds_here[...])
    speed_high = speed.astype(jnp.bfloat16).astype(jnp.float32)
    speed_mid = (speed - speed_high).astype(jnp.bfloat16).astype(jnp.float32)
    speed_low = speed - speed_high - speed_mid
    barrier = jnp.where(thermal, barriers_here[...], 0.0)
    barrier_high = barrier.astype(jnp.bfloat16).astype(jnp.float32)
    barrier_low = barrier - barrier_high
    photo = jnp.where(thermal, 0.0, 1.0)
    row = lax.broadcasted_iota(jnp.int32, (KDIM - SPAD, REAC), 0)
    extra = jnp.zeros((KDIM - SPAD, REAC), jnp.float32)
    for place, value in enumerate(
        (barrier_high, barrier_low, speed_high, speed_mid, speed_low, photo)
    ):
        extra = jnp.where(row == place, value, extra)
    turning[pl.ds(0, SPAD), used] = consuming
    turning[pl.ds(SPAD, KDIM - SPAD), used] = extra
    gather[...] = jnp.transpose(turning[...]).astype(jnp.bfloat16)

    row = lax.broadcasted_iota(jnp.int32, (KDIM - SPAD, COLS), 0)
    for layer in range(HALF):
        warmth = heat_here[pl.ds(group * HALF + layer, 1), :]
        flux = light_here[pl.ds(group * HALF + layer, 1), :]
        inverse = (1.0 / 250.0 - 1.0 / warmth) * 1.4426950408889634
        term = jnp.where(row < 2, inverse, 0.0)
        term = jnp.where((row >= 2) & (row < 5), 1.0, term)
        term = jnp.where(row == 5, lax.log2(flux), term)
        term_high, term_low = high_low(term)
        terms[0 : KDIM - SPAD, pl.ds(layer * COLS, COLS)] = term_high
        terms[KDIM - SPAD : 2 * (KDIM - SPAD), pl.ds(layer * COLS, COLS)] = term_low


def chemistry_kernel(
    tile_of,
    own,
    swapped,
    marker,
    lookup,
    weights,
    gather,
    terms,
    send,
    tendency,
    amounts,
    logs,
    start,
    now,
    sem,
):
    group, tile = tile_of[0], tile_of[1]

    @pl.when(group == 1)
    def _():
        pltpu.make_async_copy(own, amounts.at[pl.ds(0, ROWS)], sem).start()

    @pl.when(group == 0)
    def _():
        pltpu.make_async_copy(swapped, amounts.at[pl.ds(0, ROWS)], sem).start()

    lit = jnp.max(marker[pl.ds(tile, 1), :])
    sweeps = jnp.where(lit > 0, ITER_DAY, ITER_NIGHT)
    extra = KDIM - SPAD
    dark = (lax.broadcasted_iota(jnp.int32, (extra, CELLS), 0) == 5) & (lit <= 0)
    for place, value in ((SPAD, DARK), (KDIM + SPAD, 0.0)):
        term = terms[pl.ds(0 if place == SPAD else extra, extra), :].astype(jnp.float32)
        logs[pl.ds(place, extra), :] = jnp.where(dark, value, term).astype(jnp.bfloat16)
    amounts[pl.ds(ROWS, SPAD * LAYERS - ROWS), :] = jnp.ones(
        (SPAD * LAYERS - ROWS, COLS), jnp.float32
    )
    pltpu.make_async_copy(own, amounts.at[pl.ds(0, ROWS)], sem).wait()
    for layer in range(HALF):
        begin = amounts[pl.ds(group * HALF + layer, SPAD, stride=LAYERS), :]
        start[:, pl.ds(layer * COLS, COLS)] = begin
        now[:, pl.ds(layer * COLS, COLS)] = begin

    chunks = [pl.ds(at, CHUNK) for at in range(0, CELLS, CHUNK)]

    @pl.loop(0, sweeps)
    def _(_):
        for cells in chunks:
            log_high, log_low = high_low(lax.log2(now[:, cells]))
            logs[0:SPAD, cells] = log_high
            logs[KDIM : KDIM + SPAD, cells] = log_low
        for cells in chunks:
            rate = jnp.exp2(
                dot(gather[...], logs[0:KDIM, cells]) + dot(gather[...], logs[KDIM:, cells])
            )
            high, low = high_low(rate)
            both = dot(weights[0 : 2 * SPAD], high) + dot(weights[0 : 2 * SPAD], low)
            gain = both[SPAD:] + dot(weights[2 * SPAD :], high)
            concen = now[:, cells]
            now[:, cells] = concen * (start[:, cells] + gain) / (concen + both[:SPAD])

    lane = lax.broadcasted_iota(jnp.int32, (COLS, COLS), 1)
    column = jnp.sum(jnp.where(lane == tile, lookup[...], 0), axis=1, keepdims=True)
    pick = jnp.where(lane == column - tile * COLS, 1.0, 0.0)
    ordered = jnp.where(lane == tile_at(lax.broadcasted_iota(jnp.int32, (COLS, COLS), 0)), 1.0, 0.0)
    choose = dot(ordered.astype(jnp.bfloat16), pick.astype(jnp.bfloat16)).astype(jnp.bfloat16)
    for layer in range(HALF):
        cells = pl.ds(layer * COLS, COLS)
        solved = now[:, cells]
        tendency[pl.ds(layer * SPAD, SPAD), :] = solved - start[:, cells]
        rest = jnp.concatenate([solved, jnp.zeros((KDIM - SPAD, COLS), jnp.float32)], axis=0)
        parts = []
        for _ in range(3):
            part = rest.astype(jnp.bfloat16)
            rest = rest - part.astype(jnp.float32)
            parts.append(across(choose, part))
        turned = parts[0] + parts[1] + parts[2]
        for half in range(2):
            send[pl.ds(2 * layer + half, COLS, stride=LAYERS), :] = turned[
                :, half * COLS : (half + 1) * COLS
            ]


def across(a, b):
    return lax.dot_general(a, b, (((1,), (1,)), ((), ())), preferred_element_type=jnp.float32)


def edge_kernel(tracers, wind, packed, padded):
    row = lax.broadcasted_iota(jnp.int32, (2 * EDGE, COLS), 0)
    column = lax.broadcasted_iota(jnp.int32, (2 * EDGE, COLS), 1)
    pick = jnp.where(column == (row + COLS - EDGE) % COLS, 1.0, 0.0).astype(jnp.bfloat16)
    for layer in range(LAYERS):
        padded[layer, SPEC - 4 :, :] = jnp.zeros((KDIM - SPEC + 4, COLS), jnp.float32)
        padded[layer, 0:SPEC, :] = tracers[pl.ds(layer, SPEC, stride=LAYERS), :]
        padded[layer, SPEC : SPEC + 1, :] = wind[layer : layer + 1, :]
    for layer in range(LAYERS):
        high, low = high_low(padded[layer])
        packed[pl.ds(layer * 2 * EDGE, 2 * EDGE), :] = across(pick, high) + across(pick, low)


def advect(tile, tracers, wind, from_low, from_high, own_tend, other_tend, state):
    sides = 2 * EDGE * LAYERS
    low_part = lax.broadcasted_iota(jnp.int32, (sides, KDIM), 0) % (2 * EDGE) < EDGE
    low_there = jnp.where(tile > 0, 1.0, 0.0)
    high_there = jnp.where(tile < COLS - 1, 1.0, 0.0)
    beside = jnp.where(low_part, from_low[...] * low_there, from_high[...] * high_there)
    beside = jnp.concatenate([beside, jnp.zeros((COLS - sides, KDIM), jnp.float32)], axis=0)
    beside = jnp.transpose(beside)
    wind_row = jnp.broadcast_to(beside[SPEC : SPEC + 1, :], (LAYERS, COLS))
    layer_of = lax.broadcasted_iota(jnp.int32, (LAYERS, COLS), 0)
    wind_side = jnp.zeros((LAYERS, COLS), jnp.float32)
    for layer in range(LAYERS):
        moved = pltpu.roll(wind_row, (COLS - EDGE - 2 * EDGE * layer) % COLS, 1)
        wind_side = jnp.where(layer_of == layer, moved, wind_side)

    lane = lax.broadcasted_iota(jnp.int32, (LAYERS, COLS), 1)
    lowest, highest = lane == 0, lane == COLS - 1

    def left(pair):
        up = [pltpu.roll(v, 1, 1) for v in pair]
        return jnp.where(lowest, up[1], up[0]), jnp.where(lowest, up[0], up[1])

    def right(pair):
        down = [pltpu.roll(v, COLS - 1, 1) for v in pair]
        return jnp.where(highest, down[1], down[0]), jnp.where(highest, down[0], down[1])

    factors = [
        (0.5 * c * (1.0 + c), 1.0 - c * c, 0.5 * c * (c - 1.0)) for c in (wind[...], wind_side)
    ]
    one = jnp.ones((LAYERS, COLS), jnp.float32)
    band = {0: (one, one)}
    for _ in range(ADV_STEPS):
        lefts = {d: left(pair) for d, pair in band.items()}
        rights = {d: right(pair) for d, pair in band.items()}
        reach = max(band) + 1
        fresh = {}
        for d in range(-reach, reach + 1):
            total = [0.0, 0.0]
            for source, factor in ((lefts.get(d + 1), 0), (band.get(d), 1), (rights.get(d - 1), 2)):
                if source is not None:
                    total = [t + factors[i][factor] * source[i] for i, t in enumerate(total)]
            fresh[d] = tuple(total)
        band = fresh

    rows = lax.broadcasted_iota(jnp.int32, (KDIM, COLS), 0)
    extra = rows - COLS
    edge = extra % (2 * EDGE)
    place = jnp.where(rows < COLS, rows, jnp.where(edge < EDGE, edge - EDGE, edge - EDGE + COLS))
    offset = place - lax.broadcasted_iota(jnp.int32, (KDIM, COLS), 1)
    beside_high, beside_low = high_low(beside[:SPAD])
    for layer in range(LAYERS):
        here = (rows < COLS) | (extra // (2 * EDGE) == layer)
        matrix = jnp.zeros((KDIM, COLS), jnp.float32)
        for d, (weight, _) in band.items():
            matrix = jnp.where(offset == d, weight[layer : layer + 1, :], matrix)
        matrix_high, matrix_low = high_low(jnp.where(here, matrix, 0.0))
        main = jnp.concatenate(
            [
                tracers[pl.ds(layer, SPEC, stride=LAYERS), :],
                jnp.zeros((SPAD - SPEC, COLS), jnp.float32),
            ],
            axis=0,
        )
        main_high, main_low = high_low(main)
        high = jnp.concatenate([main_high, beside_high], axis=1)
        low = jnp.concatenate([main_low, beside_low], axis=1)
        moved = dot(high, matrix_high) + dot(low, matrix_high) + dot(high, matrix_low)
        tend = own_tend if layer < HALF else other_tend
        state[pl.ds(layer, SPEC, stride=LAYERS), :] = (
            moved[:SPEC] + tend[pl.ds(layer % HALF * SPAD, SPEC), :]
        )


def owner_result(own, other, state):
    order = place_of(lax.broadcasted_iota(jnp.int32, (COLS, COLS), 1))
    for block, begin in ((own, HALF), (other, 0)):
        for layer in range(HALF):
            for half in range(2):
                count = min(COLS, SPEC - half * COLS)
                turned = jnp.transpose(block[pl.ds(2 * layer + half, COLS, stride=LAYERS), :])
                turned = jnp.take_along_axis(turned, order, axis=1)
                state[pl.ds(half * COLS * LAYERS + begin + layer, count, stride=LAYERS), :] = (
                    turned[:count]
                )


def final_kernel(
    tile_of, tracers, wind, from_low, from_high, own_tend, other_tend, own, other, state
):
    @pl.when(tile_of[0] == 0)
    def _():
        advect(tile_of[1], tracers, wind, from_low, from_high, own_tend, other_tend, state)

    @pl.when(tile_of[0] == 1)
    def _():
        owner_result(own, other, state)


def cost(microseconds):
    return pl.CostEstimate(
        flops=int(microseconds * 1e9), bytes_accessed=int(microseconds * 2e6), transcendentals=0
    )


def bf16(*shape):
    return jax.ShapeDtypeStruct(shape, jnp.bfloat16)


def f32(*shape):
    return jax.ShapeDtypeStruct(shape, jnp.float32)


def local(
    species_amounts,
    air_warmth_kelvin,
    sunlight_strength,
    wind_stability_numbers,
    illuminated_marker,
    position_vertical_lookup,
    speed_constants,
    barrier_kelvins,
    consumed_species,
    outcome_species,
    outcome_fractions,
):
    tile_of = jnp.stack([lax.axis_index("group"), lax.axis_index("tile")]).astype(jnp.int32)
    amounts = species_amounts.reshape(ROWS, COLS)
    swap = [(0, 1), (1, 0)]
    swapped = lax.ppermute(amounts, "group", swap)

    weights, gather, terms = pl.pallas_call(
        prepare_kernel,
        out_shape=(
            bf16(3 * SPAD, RPAD),
            bf16(RPAD, KDIM),
            bf16(2 * (KDIM - SPAD), CELLS),
        ),
        in_specs=[SMEM] + [HBM] * 7,
        out_specs=(VMEM, VMEM, VMEM),
        scratch_shapes=[
            pltpu.VMEM((LAYERS, COLS), jnp.float32),
            pltpu.VMEM((LAYERS, COLS), jnp.float32),
            pltpu.VMEM((2, REAC), jnp.int32),
            pltpu.VMEM((2, REAC), jnp.int32),
            pltpu.VMEM((2, REAC), jnp.float32),
            pltpu.VMEM((1, REAC), jnp.float32),
            pltpu.VMEM((1, REAC), jnp.float32),
            pltpu.VMEM((KDIM, RPAD), jnp.float32),
            pltpu.SemaphoreType.DMA((7,)),
        ],
        compiler_params=PARAMS,
        cost_estimate=cost(1),
        name="prepare",
    )(
        tile_of,
        air_warmth_kelvin,
        sunlight_strength,
        consumed_species,
        outcome_species,
        outcome_fractions,
        speed_constants.reshape(1, REAC),
        barrier_kelvins.reshape(1, REAC),
    )
    send, tendency = pl.pallas_call(
        chemistry_kernel,
        out_shape=(f32(COLS * LAYERS, COLS), f32(HALF * SPAD, COLS)),
        in_specs=[SMEM, ANY, ANY] + [VMEM] * 5,
        out_specs=(VMEM, VMEM),
        scratch_shapes=[
            pltpu.VMEM((SPAD * LAYERS, COLS), jnp.float32),
            pltpu.VMEM((2 * KDIM, CELLS), jnp.bfloat16),
            pltpu.VMEM((SPAD, CELLS), jnp.float32),
            pltpu.VMEM((SPAD, CELLS), jnp.float32),
            pltpu.SemaphoreType.DMA(()),
        ],
        compiler_params=PARAMS,
        cost_estimate=cost(6),
        name="chemistry",
    )(
        tile_of,
        amounts,
        swapped,
        illuminated_marker.reshape(COLS, COLS),
        position_vertical_lookup.reshape(COLS, COLS),
        weights,
        gather,
        terms,
    )
    received = lax.all_to_all(
        send.reshape(COLS, LAYERS, COLS),
        "tile",
        split_axis=0,
        concat_axis=0,
        axis_index_groups=[ORDER],
        tiled=True,
    )

    edges = pl.pallas_call(
        edge_kernel,
        out_shape=f32(2 * EDGE * LAYERS, KDIM),
        in_specs=[VMEM, VMEM],
        out_specs=VMEM,
        scratch_shapes=[pltpu.VMEM((LAYERS, KDIM, COLS), jnp.float32)],
        compiler_params=PARAMS,
        cost_estimate=cost(1),
        name="edges",
    )(amounts, wind_stability_numbers)
    count = lax.axis_size("tile")
    from_low = lax.ppermute(edges, "tile", [(i, (i + 1) % count) for i in range(count)])
    from_high = lax.ppermute(edges, "tile", [((i + 1) % count, i) for i in range(count)])
    other_tendency = lax.ppermute(tendency, "group", swap)
    received, from_low, from_high, other_tendency = lax.optimization_barrier(
        (received, from_low, from_high, other_tendency)
    )
    received = received.reshape(COLS * LAYERS, COLS)
    other_received = lax.ppermute(received, "group", swap)
    state = pl.pallas_call(
        final_kernel,
        out_shape=f32(ROWS, COLS),
        in_specs=[SMEM] + [VMEM] * 8,
        out_specs=VMEM,
        compiler_params=PARAMS,
        cost_estimate=cost(2),
        name="final",
    )(
        tile_of,
        amounts,
        wind_stability_numbers,
        from_low,
        from_high,
        tendency,
        other_tendency,
        received,
        other_received,
    )
    return state.reshape(1, SPEC, LAYERS, COLS)


def solution(mesh):
    return jax.shard_map(
        local,
        mesh=mesh,
        in_specs=(
            P("group", None, None, "tile"),
            P(None, "tile"),
            P(None, "tile"),
            P(None, "tile"),
            P(),
            P(),
            P(),
            P(),
            P(),
            P(),
            P(),
        ),
        out_specs=P("group", None, None, "tile"),
        check_vma=False,
    )
```

profile of v0, /device:TPU:1, one launch (start us, length us, event | category | flops | bytes accessed | tf_op | source)
XLA Modules:
  0.0 46.6 jit_solution(2978642392762500565)
XLA Ops:
  0.0 0.0 copy-start.9
  0.0 3.2 %collective-permute-start = (f32[1760,128]{1,0:T(8,128)}, f32[1760,128]{1,0:T(8,128)S(1)}, u32[]{:S(2)}, u32[]{:S(2)}) collective-permute-start(f32[1760,128]{1,0:T(8,128)} %bitcast.12), channel_id=1, source_target_pairs={{0,128},{128,0},{1,129},{129,1},{2,130},{130,2},{3,131},{131,3},{4... | collective-permute-start | bytes 2703368 | tf_op jit(solution)/shard_map/ppermute | solution.py:374
  3.2 0.0 copy-start.7
  3.2 0.0 copy-start.6
  3.2 0.0 copy-start.5
  3.2 0.0 copy-start.4
  3.3 0.0 copy-start.3
  3.3 0.1 pad_add_fusion.tile_of
  3.3 0.0 copy-done.9
  3.3 0.6 %copy-done.7 = f32[2,500]{1,0:T(2,128)S(1)} copy-done((f32[2,500]{1,0:T(2,128)S(1)}, f32[2,500]{1,0:T(2,128)}, u32[]{:S(2)}) %copy-start.7) | copy-done | bytes 4024
  3.9 0.0 copy-done.6
  3.9 0.0 copy-done.5
  4.0 0.0 copy-done.4
  4.0 0.0 copy-done.3
  4.0 0.0 copy-start.10
  4.0 0.7 %copy-done.10 = f32[500]{0:T(512)S(1)} copy-done((f32[500]{0:T(512)S(1)}, f32[500]{0:T(512)}, u32[]{:S(2)}) %copy-start.10) | copy-done | bytes 2024
  4.7 0.0 copy-start
  4.7 0.0 copy-start.1
  4.7 0.0 copy-start.2
  4.7 1.1 %prepare.1 = (bf16[672,512]{1,0:T(8,128)(2,1)S(1)}, bf16[512,256]{1,0:T(8,128)(2,1)S(1)}, bf16[64,512]{1,0:T(8,128)(2,1)S(1)}) custom-call(s32[2]{0:T(128)S(1)} %pad_add_fusion.tile_of, f32[8,128]{1,0:T(8,128)S(1)} %copy-done.3, f32[8,128]{1,0:T(8,128)S(1)} %copy-done.4, s32[2,500]{1,0:T(2,128)S(1)} %copy-done.5, s32[2,500]{1,0:T(2,128)S(1)} %copy-done.6, ...), custom_call_target="tpu_custom_call" | custom-call | flops 1000000000 | bytes 2000000 | tf_op jit(solution)/shard_map/prepare/pallas_call | solution.py:376
  5.8 0.0 collective-permute-done.swapped
  5.8 0.1 copy-done
  5.9 0.0 copy-done.1
  5.9 0.0 copy-done.2
  5.9 4.9 %chemistry.1 = (f32[1024,128]{1,0:T(8,128)}, f32[896,128]{1,0:T(8,128)S(1)}) custom-call(s32[2]{0:T(128)S(1)} %pad_add_fusion.tile_of, f32[1760,128]{1,0:T(8,128)S(1)} %bitcast.13, f32[1760,128]{1,0:T(8,128)S(1)} %collective-permute-done.swapped, s32[128,128]{1,0:T(8,128)S(1)} %bitcast.16, s32[128,128]{1,0:T(8,128)S(1)} %bitcast.17, ...), custom_call_target="tpu_custom_call" | custom-call | flops 6000000000 | bytes 12000000 | tf_op jit(solution)/shard_map/chemistry/pallas_call | solution.py:409
  10.7 0.0 copy-start.8
  10.7 17.3 %all-to-all-start = ((f32[128,8,128]{2,1,0:T(8,128)}), f32[128,8,128]{2,1,0:T(8,128)S(1)}, u32[]{:S(2)}, u32[]{:S(2)}) async-start(f32[128,8,128]{2,1,0:T(8,128)} %bitcast.7), calls=%async_computation | async-start | bytes 1048576 | tf_op jit(solution)/shard_map/all_to_all | solution.py:434
  28.1 0.7 %collective-permute-start.3 = (f32[896,128]{1,0:T(8,128)S(1)}, f32[896,128]{1,0:T(8,128)S(1)}, u32[]{:S(2)}, u32[]{:S(2)}) collective-permute-start(f32[896,128]{1,0:T(8,128)S(1)} %get-tuple-element.18.own_tend), channel_id=1, source_target_pairs={{0,128},{128,0},{1,129},{129,1},{2,130},{130,2},{3,131},{131,3},{4... | collective-permute-start | bytes 1376264 | tf_op jit(solution)/shard_map/ppermute | solution.py:456
  28.8 0.0 copy-done.8
  28.8 0.4 edges.1
  29.2 0.6 %collective-permute-start.1 = (f32[64,256]{1,0:T(8,128)S(1)}, f32[64,256]{1,0:T(8,128)S(1)}, u32[]{:S(2)}, u32[]{:S(2)}) collective-permute-start(f32[64,256]{1,0:T(8,128)S(1)} %edges.1), channel_id=1, source_target_pairs={{0,1},{1,2},{2,3},{3,4},{4,5},{5,6},{6,7},{7,8},{8,9},{9,10},{10,1... | collective-permute-start | bytes 196616 | tf_op jit(solution)/shard_map/ppermute | solution.py:454
  29.8 6.3 %collective-permute-start.2 = (f32[64,256]{1,0:T(8,128)S(1)}, f32[64,256]{1,0:T(8,128)S(1)}, u32[]{:S(2)}, u32[]{:S(2)}) collective-permute-start(f32[64,256]{1,0:T(8,128)S(1)} %edges.1), channel_id=1, source_target_pairs={{1,0},{2,1},{3,2},{4,3},{5,4},{6,5},{7,6},{8,7},{9,8},{10,9},{11,1... | collective-permute-start | bytes 196616 | tf_op jit(solution)/shard_map/ppermute | solution.py:455
  36.1 4.5 %collective-permute-done.1.from_low = f32[64,256]{1,0:T(8,128)S(1)} collective-permute-done((f32[64,256]{1,0:T(8,128)S(1)}, f32[64,256]{1,0:T(8,128)S(1)}, u32[]{:S(2)}, u32[]{:S(2)}) %collective-permute-start.1) | collective-permute-done | bytes 65568 | tf_op jit(solution)/shard_map/ppermute | solution.py:454
  40.6 0.0 collective-permute-done.2.from_high
  40.6 0.0 collective-permute-done.3.other_tend
  40.6 0.4 all-to-all-done
  41.0 1.8 %collective-permute-start.4 = (f32[1024,128]{1,0:T(8,128)S(1)}, f32[1024,128]{1,0:T(8,128)S(1)}, u32[]{:S(2)}, u32[]{:S(2)}) collective-permute-start(f32[1024,128]{1,0:T(8,128)S(1)} %bitcast.10), channel_id=1, source_target_pairs={{0,128},{128,0},{1,129},{129,1},{2,130},{130,2},{3,131},{131,3},{4... | collective-permute-start | bytes 1572872 | tf_op jit(solution)/shard_map/ppermute | solution.py:461
  42.9 1.5 %collective-permute-done.4.other = f32[1024,128]{1,0:T(8,128)S(1)} collective-permute-done((f32[1024,128]{1,0:T(8,128)S(1)}, f32[1024,128]{1,0:T(8,128)S(1)}, u32[]{:S(2)}, u32[]{:S(2)}) %collective-permute-start.4) | collective-permute-done | bytes 524320 | tf_op jit(solution)/shard_map/ppermute | solution.py:461
  44.4 2.2 %final.1 = f32[1760,128]{1,0:T(8,128)} custom-call(s32[2]{0:T(128)S(1)} %pad_add_fusion.tile_of, f32[1760,128]{1,0:T(8,128)S(1)} %bitcast.15, f32[8,128]{1,0:T(8,128)S(1)} %copy-done.8, f32[64,256]{1,0:T(8,128)S(1)} %collective-permute-done.1.from_low, f32[64,256]{1,0:T(8,128)S(1)} %collective-permute-done.2.from_high, ...), custom_call_target="tpu_custom_call" | custom-call | flops 2000000000 | bytes 4000000 | tf_op jit(solution)/shard_map/final/pallas_call | solution.py:462
Async XLA Ops:
  0.0 3.3 %copy-start.9 = (f32[500]{0:T(512)S(1)}, f32[500]{0:T(512)}, u32[]{:S(2)}) copy-start(f32[500]{0:T(512)} %param.17) | copy-start | bytes 6004
  0.0 5.8 %collective-permute-start = (f32[1760,128]{1,0:T(8,128)}, f32[1760,128]{1,0:T(8,128)S(1)}, u32[]{:S(2)}, u32[]{:S(2)}) collective-permute-start(f32[1760,128]{1,0:T(8,128)} %bitcast.12), channel_id=1, source_target_pairs={{0,128},{128,0},{1,129},{129,1},{2,130},{130,2},{3,131},{131,3},{4... | collective-permute-start | bytes 2703368 | tf_op jit(solution)/shard_map/ppermute | solution.py:374
  3.2 0.7 %copy-start.7 = (f32[2,500]{1,0:T(2,128)S(1)}, f32[2,500]{1,0:T(2,128)}, u32[]{:S(2)}) copy-start(f32[2,500]{1,0:T(2,128)} %fractions.1) | copy-start | bytes 12004
  3.2 0.7 %copy-start.6 = (s32[2,500]{1,0:T(2,128)S(1)}, s32[2,500]{1,0:T(2,128)}, u32[]{:S(2)}) copy-start(s32[2,500]{1,0:T(2,128)} %outcome.1) | copy-start | bytes 12004
  3.2 0.7 %copy-start.5 = (s32[2,500]{1,0:T(2,128)S(1)}, s32[2,500]{1,0:T(2,128)}, u32[]{:S(2)}) copy-start(s32[2,500]{1,0:T(2,128)} %consumed.1) | copy-start | bytes 12004
  3.2 0.7 %copy-start.4 = (f32[8,128]{1,0:T(8,128)S(1)}, f32[8,128]{1,0:T(8,128)}, u32[]{:S(2)}) copy-start(f32[8,128]{1,0:T(8,128)} %light.1) | copy-start | bytes 12292
  3.3 0.7 %copy-start.3 = (f32[8,128]{1,0:T(8,128)S(1)}, f32[8,128]{1,0:T(8,128)}, u32[]{:S(2)}) copy-start(f32[8,128]{1,0:T(8,128)} %heat.1) | copy-start | bytes 12292
  4.0 0.7 %copy-start.10 = (f32[500]{0:T(512)S(1)}, f32[500]{0:T(512)}, u32[]{:S(2)}) copy-start(f32[500]{0:T(512)} %param.18) | copy-start | bytes 6004
  4.7 1.2 %copy-start = (f32[1,220,8,128]{3,2,1,0:T(8,128)S(1)}, f32[1,220,8,128]{3,2,1,0:T(8,128)}, u32[]{:S(2)}) copy-start(f32[1,220,8,128]{3,2,1,0:T(8,128)} %param.11) | copy-start | bytes 2703364
  4.7 1.2 %copy-start.1 = (s32[16384]{0:T(1024)S(1)}, s32[16384]{0:T(1024)}, u32[]{:S(2)}) copy-start(s32[16384]{0:T(1024)} %param.15) | copy-start | bytes 196612
  4.7 1.2 %copy-start.2 = (s32[16384]{0:T(1024)S(1)}, s32[16384]{0:T(1024)}, u32[]{:S(2)}) copy-start(s32[16384]{0:T(1024)} %param.16) | copy-start | bytes 196612
  10.7 18.1 %copy-start.8 = (f32[8,128]{1,0:T(8,128)S(1)}, f32[8,128]{1,0:T(8,128)}, u32[]{:S(2)}) copy-start(f32[8,128]{1,0:T(8,128)} %wind.3) | copy-start | bytes 12292
  10.7 30.3 %all-to-all-start = ((f32[128,8,128]{2,1,0:T(8,128)}), f32[128,8,128]{2,1,0:T(8,128)S(1)}, u32[]{:S(2)}, u32[]{:S(2)}) async-start(f32[128,8,128]{2,1,0:T(8,128)} %bitcast.7), calls=%async_computation | async-start | bytes 1048576 | tf_op jit(solution)/shard_map/all_to_all | solution.py:434
  28.1 12.5 %collective-permute-start.3 = (f32[896,128]{1,0:T(8,128)S(1)}, f32[896,128]{1,0:T(8,128)S(1)}, u32[]{:S(2)}, u32[]{:S(2)}) collective-permute-start(f32[896,128]{1,0:T(8,128)S(1)} %get-tuple-element.18.own_tend), channel_id=1, source_target_pairs={{0,128},{128,0},{1,129},{129,1},{2,130},{130,2},{3,131},{131,3},{4... | collective-permute-start | bytes 1376264 | tf_op jit(solution)/shard_map/ppermute | solution.py:456
  29.2 11.4 %collective-permute-start.1 = (f32[64,256]{1,0:T(8,128)S(1)}, f32[64,256]{1,0:T(8,128)S(1)}, u32[]{:S(2)}, u32[]{:S(2)}) collective-permute-start(f32[64,256]{1,0:T(8,128)S(1)} %edges.1), channel_id=1, source_target_pairs={{0,1},{1,2},{2,3},{3,4},{4,5},{5,6},{6,7},{7,8},{8,9},{9,10},{10,1... | collective-permute-start | bytes 196616 | tf_op jit(solution)/shard_map/ppermute | solution.py:454
  29.8 10.8 %collective-permute-start.2 = (f32[64,256]{1,0:T(8,128)S(1)}, f32[64,256]{1,0:T(8,128)S(1)}, u32[]{:S(2)}, u32[]{:S(2)}) collective-permute-start(f32[64,256]{1,0:T(8,128)S(1)} %edges.1), channel_id=1, source_target_pairs={{1,0},{2,1},{3,2},{4,3},{5,4},{6,5},{7,6},{8,7},{9,8},{10,9},{11,1... | collective-permute-start | bytes 196616 | tf_op jit(solution)/shard_map/ppermute | solution.py:455
  41.0 3.4 %collective-permute-start.4 = (f32[1024,128]{1,0:T(8,128)S(1)}, f32[1024,128]{1,0:T(8,128)S(1)}, u32[]{:S(2)}, u32[]{:S(2)}) collective-permute-start(f32[1024,128]{1,0:T(8,128)S(1)} %bitcast.10), channel_id=1, source_target_pairs={{0,128},{128,0},{1,129},{129,1},{2,130},{130,2},{3,131},{131,3},{4... | collective-permute-start | bytes 1572872 | tf_op jit(solution)/shard_map/ppermute | solution.py:461
where the time goes:
time: 46.7 us; the launch traced here: 46.6 us
  starting transfers between devices  30 us (64%)
  Pallas kernels  8.5 us (18%)
  waiting for transfers between devices  6.47 us (14%)
  local copies, waits for them, and re-layouts  1.43 us (3%)
    all_to_all x1, starting transfers between devices, local(): lax.all_to_all(send.reshape(COLS, LAYERS, COLS), 'tile', split_axis=0, co...  17.3 us
    ppermute x1, starting transfers between devices, local(): lax.ppermute(edges, 'tile', [((i + 1) % count, i) for i in range(count)])  6.32 us
    pallas_call x1, Pallas kernels, local(): pl.pallas_call(chemistry_kernel, out_shape=(f32(COLS * LAYERS, COLS), f32...  4.86 us
    ppermute x1, waiting for transfers between devices, local(): lax.ppermute(edges, 'tile', [(i, (i + 1) % count) for i in range(count)])  4.49 us
    ppermute x1, starting transfers between devices, local(): swapped = lax.ppermute(amounts, 'group', swap)  3.24 us
    pallas_call x1, Pallas kernels, local(): pl.pallas_call(final_kernel, out_shape=f32(ROWS, COLS), in_specs=[SMEM] +...  2.16 us
    ppermute x1, starting transfers between devices, local(): other_received = lax.ppermute(received, 'group', swap)  1.84 us
    ppermute x1, waiting for transfers between devices, local(): other_received = lax.ppermute(received, 'group', swap)  1.54 us
  transfers between devices with their start and end apart: 6, of which 3 were waited for; matrix products, arithmetic and copies ran while one was open for 0% of the time, Pallas kernels for 3%

commit v1 on v0

v1 whole, which is shorter than its diff:
```python
import jax
import jax.numpy as jnp
from jax import lax
from jax.experimental import pallas as pl
from jax.experimental.pallas import tpu as pltpu
from jax.sharding import PartitionSpec as P

SPEC = 220
REAC = 500
PHOT = 64
LAYERS = 8
COLS = 128
ADV_STEPS = 4
ITER_NIGHT = 2
ITER_DAY = 4

HALF = LAYERS // 2
ROWS = SPEC * LAYERS
SPAD = 224
KDIM = 256
RPAD = 512
CELLS = HALF * COLS
PIECES = 7
PACKED = PIECES * COLS
CHUNK = 256
EDGE = 4
DARK = -1024.0

MIDDLE = (4, 5, 3, 6, 2, 7, 1, 0)
ORDER = [z * 16 + x * 4 + y for y in range(3, -1, -1) for x in range(3, -1, -1) for z in MIDDLE]

VMEM = pl.BlockSpec(memory_space=pltpu.VMEM)
HBM = pl.BlockSpec(memory_space=pltpu.HBM)
PARAMS = pltpu.CompilerParams(vmem_limit_bytes=24 * 1024 * 1024)


def high_low(value):
    high = value.astype(jnp.bfloat16)
    return high, (value - high.astype(jnp.float32)).astype(jnp.bfloat16)


def dot(a, b):
    return jnp.dot(a, b, preferred_element_type=jnp.float32)


def tile_at(place):
    step = place % 8
    z = jnp.zeros_like(place)
    for at, value in enumerate(MIDDLE):
        z = jnp.where(step == at, value, z)
    return z * 16 + (3 - place // 8 % 4) * 4 + 3 - place // 32


def place_of(tile):
    z = tile // 16
    step = jnp.zeros_like(tile)
    for at, value in enumerate(MIDDLE):
        step = jnp.where(z == value, at, step)
    return (3 - tile % 4) * 32 + (3 - tile // 4 % 4) * 8 + step


def prepare_kernel(table, weights, gather, turning):
    spare = pl.ds(RPAD - COLS, COLS)
    weights[:, spare] = jnp.zeros((3 * SPAD, COLS), jnp.bfloat16)
    turning[:, spare] = jnp.zeros((KDIM, COLS), jnp.float32)
    row_of = [table[row : row + 1, :] for row in range(8)]

    used = pl.ds(0, REAC)
    species = lax.broadcasted_iota(jnp.int32, (SPAD, REAC), 0).astype(jnp.float32)
    thermal = lax.broadcasted_iota(jnp.int32, (1, REAC), 1) >= PHOT
    second = jnp.where(thermal, row_of[1], -1.0)
    consuming = jnp.where(species == row_of[0], 1.0, 0.0) + jnp.where(
        species == second, 1.0, 0.0
    )
    producing = jnp.where(species == row_of[2], row_of[4], 0.0) + jnp.where(
        species == row_of[3], row_of[5], 0.0
    )
    producing_high, producing_low = high_low(producing)
    weights[pl.ds(0, SPAD), used] = consuming.astype(jnp.bfloat16)
    weights[pl.ds(SPAD, SPAD), used] = producing_high
    weights[pl.ds(2 * SPAD, SPAD), used] = producing_low

    speed = lax.log2(row_of[6])
    speed_high = speed.astype(jnp.bfloat16).astype(jnp.float32)
    speed_mid = (speed - speed_high).astype(jnp.bfloat16).astype(jnp.float32)
    speed_low = speed - speed_high - speed_mid
    barrier = jnp.where(thermal, row_of[7], 0.0)
    barrier_high = barrier.astype(jnp.bfloat16).astype(jnp.float32)
    barrier_low = barrier - barrier_high
    photo = jnp.where(thermal, 0.0, 1.0)
    row = lax.broadcasted_iota(jnp.int32, (KDIM - SPAD, REAC), 0)
    extra = jnp.zeros((KDIM - SPAD, REAC), jnp.float32)
    for place, value in enumerate(
        (barrier_high, barrier_low, speed_high, speed_mid, speed_low, photo)
    ):
        extra = jnp.where(row == place, value, extra)
    turning[pl.ds(0, SPAD), used] = consuming
    turning[pl.ds(SPAD, KDIM - SPAD), used] = extra
    gather[...] = jnp.transpose(turning[...]).astype(jnp.bfloat16)


def chemistry_kernel(
    own,
    swapped,
    marker,
    lookup,
    heat,
    light,
    weights,
    gather,
    send,
    tendency,
    logs,
    start,
    now,
    stack,
    parts,
    packed,
    sems,
):
    group, tile = lax.axis_index("group"), lax.axis_index("tile")

    lit = jnp.max(marker[pl.ds(tile, 1), :])
    sweeps = jnp.where(lit > 0, ITER_DAY, ITER_NIGHT)
    row = lax.broadcasted_iota(jnp.int32, (KDIM - SPAD, COLS), 0)
    for layer in range(HALF):
        warmth = heat[pl.ds(group * HALF + layer, 1), :]
        flux = light[pl.ds(group * HALF + layer, 1), :]
        inverse = (1.0 / 250.0 - 1.0 / warmth) * 1.4426950408889634
        flux = jnp.where(lit > 0, lax.log2(flux), DARK)
        term = jnp.where(row < 2, inverse, 0.0)
        term = jnp.where((row >= 2) & (row < 5), 1.0, term)
        term = jnp.where(row == 5, flux, term)
        term_high, term_low = high_low(term)
        logs[SPAD:KDIM, pl.ds(layer * COLS, COLS)] = term_high
        logs[KDIM + SPAD :, pl.ds(layer * COLS, COLS)] = term_low
    for core, amounts in enumerate((swapped, own)):

        @pl.when(group == core)
        def _():
            for layer in range(HALF):
                begin = amounts[pl.ds(core * HALF + layer, SPEC, stride=LAYERS), :]
                start[0:SPEC, pl.ds(layer * COLS, COLS)] = begin

    start[SPEC:SPAD, :] = jnp.ones((SPAD - SPEC, CELLS), jnp.float32)
    now[...] = start[...]
    chunks = [pl.ds(at, CHUNK) for at in range(0, CELLS, CHUNK)]

    @pl.loop(0, sweeps)
    def _(_):
        for cells in chunks:
            log_high, log_low = high_low(lax.log2(now[:, cells]))
            logs[0:SPAD, cells] = log_high
            logs[KDIM : KDIM + SPAD, cells] = log_low
        for cells in chunks:
            rate = jnp.exp2(
                dot(gather[...], logs[0:KDIM, cells]) + dot(gather[...], logs[KDIM:, cells])
            )
            high, low = high_low(rate)
            both = dot(weights[0 : 2 * SPAD], high) + dot(weights[0 : 2 * SPAD], low)
            gain = both[SPAD:] + dot(weights[2 * SPAD :], high)
            concen = now[:, cells]
            now[:, cells] = concen * (start[:, cells] + gain) / (concen + both[:SPAD])

    lane = lax.broadcasted_iota(jnp.int32, (COLS, COLS), 1)
    column = jnp.sum(jnp.where(lane == tile, lookup[...], 0), axis=1, keepdims=True)
    pick = jnp.where(lane == column - tile * COLS, 1.0, 0.0)
    ordered = jnp.where(lane == tile_at(lax.broadcasted_iota(jnp.int32, (COLS, COLS), 0)), 1.0, 0.0)
    choose = dot(ordered.astype(jnp.bfloat16), pick.astype(jnp.bfloat16)).astype(jnp.bfloat16)
    for layer in range(HALF):
        cells = pl.ds(layer * COLS, COLS)
        stack[pl.ds(layer, SPEC, stride=HALF), :] = now[0:SPEC, cells]
    stack[HALF * SPEC :, :] = jnp.zeros((PACKED - HALF * SPEC, COLS), jnp.float32)
    for piece in range(PIECES):
        rest = jnp.transpose(stack[pl.ds(piece * COLS, COLS), :])
        for part in range(3):
            rounded = rest.astype(jnp.bfloat16)
            rest = rest - rounded.astype(jnp.float32)
            parts[pl.ds(part * COLS, COLS), pl.ds(piece * COLS, COLS)] = rounded
    copies = []
    for half in range(2):
        owners = COLS // 2
        turned = dot(
            jnp.concatenate([choose[half * owners : (half + 1) * owners]] * 3, axis=1), parts[...]
        )
        for piece in range(PIECES):
            packed[pl.ds(half * owners * PIECES + piece, owners, stride=PIECES), :] = turned[
                :, piece * COLS : (piece + 1) * COLS
            ]
        rows = pl.ds(half * owners * PIECES, owners * PIECES)
        copies.append(pltpu.make_async_copy(packed.at[rows], send.at[rows], sems.at[half]))
        copies[half].start()
    for layer in range(HALF):
        cells = pl.ds(layer * COLS, COLS)
        tendency[pl.ds(layer * SPAD, SPAD), :] = now[:, cells] - start[:, cells]
    for copy in copies:
        copy.wait()


def across(a, b):
    return lax.dot_general(a, b, (((1,), (1,)), ((), ())), preferred_element_type=jnp.float32)


def edge_kernel(tracers, wind, to_low, to_high, padded):
    row = lax.broadcasted_iota(jnp.int32, (2 * EDGE, COLS), 0)
    column = lax.broadcasted_iota(jnp.int32, (2 * EDGE, COLS), 1)
    pick = jnp.where(column == (row + COLS - EDGE) % COLS, 1.0, 0.0).astype(jnp.bfloat16)
    for layer in range(LAYERS):
        padded[layer, SPEC - 4 :, :] = jnp.zeros((KDIM - SPEC + 4, COLS), jnp.float32)
        padded[layer, 0:SPEC, :] = tracers[pl.ds(layer, SPEC, stride=LAYERS), :]
        padded[layer, SPEC : SPEC + 1, :] = wind[layer : layer + 1, :]
    for layer in range(LAYERS):
        high, low = high_low(padded[layer])
        picked = across(pick, high) + across(pick, low)
        to_high[pl.ds(layer * EDGE, EDGE), :] = picked[:EDGE]
        to_low[pl.ds(layer * EDGE, EDGE), :] = picked[EDGE:]


def advect(tracers, wind, from_low, from_high, own_tend, other_tend, state, after):
    tile = lax.axis_index("tile")
    side = EDGE * LAYERS
    low_there = jnp.where(tile > 0, 1.0, 0.0)
    high_there = jnp.where(tile < COLS - 1, 1.0, 0.0)
    beside = jnp.concatenate(
        [
            from_low[...] * low_there,
            from_high[...] * high_there,
            jnp.zeros((COLS - 2 * side, KDIM), jnp.float32),
        ],
        axis=0,
    )
    beside = jnp.transpose(beside)
    wind_row = jnp.broadcast_to(beside[SPEC : SPEC + 1, :], (LAYERS, COLS))
    layer_of = lax.broadcasted_iota(jnp.int32, (LAYERS, COLS), 0)
    right_half = lax.broadcasted_iota(jnp.int32, (LAYERS, COLS), 1) >= COLS // 2
    wind_side = jnp.zeros((LAYERS, COLS), jnp.float32)
    for layer in range(LAYERS):
        low = pltpu.roll(wind_row, COLS - EDGE - EDGE * layer, 1)
        high = pltpu.roll(wind_row, COLS - side - EDGE * layer, 1)
        wind_side = jnp.where(layer_of == layer, jnp.where(right_half, low, high), wind_side)

    lane = lax.broadcasted_iota(jnp.int32, (LAYERS, COLS), 1)
    lowest, highest = lane == 0, lane == COLS - 1

    def left(pair):
        up = [pltpu.roll(v, 1, 1) for v in pair]
        return jnp.where(lowest, up[1], up[0]), jnp.where(lowest, up[0], up[1])

    def right(pair):
        down = [pltpu.roll(v, COLS - 1, 1) for v in pair]
        return jnp.where(highest, down[1], down[0]), jnp.where(highest, down[0], down[1])

    factors = [
        (0.5 * c * (1.0 + c), 1.0 - c * c, 0.5 * c * (c - 1.0)) for c in (wind[...], wind_side)
    ]
    one = jnp.ones((LAYERS, COLS), jnp.float32)
    band = {0: (one, one)}
    for _ in range(ADV_STEPS):
        lefts = {d: left(pair) for d, pair in band.items()}
        rights = {d: right(pair) for d, pair in band.items()}
        reach = max(band) + 1
        fresh = {}
        for d in range(-reach, reach + 1):
            total = [0.0, 0.0]
            for source, factor in ((lefts.get(d + 1), 0), (band.get(d), 1), (rights.get(d - 1), 2)):
                if source is not None:
                    total = [t + factors[i][factor] * source[i] for i, t in enumerate(total)]
            fresh[d] = tuple(total)
        band = fresh

    rows = lax.broadcasted_iota(jnp.int32, (KDIM, COLS), 0)
    extra = rows - COLS
    edge = extra % EDGE
    place = jnp.where(rows < COLS, rows, jnp.where(extra < side, edge - EDGE, edge + COLS))
    offset = place - lax.broadcasted_iota(jnp.int32, (KDIM, COLS), 1)
    beside_high, beside_low = high_low(beside[:SPAD])
    for layer in range(LAYERS):
        here = (rows < COLS) | (extra % side // EDGE == layer)
        matrix = jnp.zeros((KDIM, COLS), jnp.float32)
        for d, (weight, _) in band.items():
            matrix = jnp.where(offset == d, weight[layer : layer + 1, :], matrix)
        matrix_high, matrix_low = high_low(jnp.where(here, matrix, 0.0))
        main = jnp.concatenate(
            [
                tracers[pl.ds(layer, SPEC, stride=LAYERS), :],
                jnp.zeros((SPAD - SPEC, COLS), jnp.float32),
            ],
            axis=0,
        )
        main_high, main_low = high_low(main)
        high = jnp.concatenate([main_high, beside_high], axis=1)
        low = jnp.concatenate([main_low, beside_low], axis=1)
        moved = dot(high, matrix_high) + dot(low, matrix_high) + dot(high, matrix_low)
        tend = own_tend if layer < HALF else other_tend
        state[pl.ds(layer, SPEC, stride=LAYERS), :] = (
            moved[:SPEC] + tend[pl.ds(layer % HALF * SPAD, SPEC), :]
        )
        after(layer)


def unpack(block, stack, state, begin, after):
    order = place_of(lax.broadcasted_iota(jnp.int32, (COLS, COLS), 1))
    for piece in range(PIECES):
        turned = jnp.transpose(block[pl.ds(piece, COLS, stride=PIECES), :])
        stack[pl.ds(piece * COLS, COLS), :] = jnp.take_along_axis(turned, order, axis=1)
        first, count = slab(piece)
        for layer in range(HALF):
            state[pl.ds(first * LAYERS + begin + layer, count, stride=LAYERS), :] = stack[
                pl.ds(piece * COLS + layer, count, stride=HALF), :
            ]
        after(piece)


def slab(piece):
    first = piece * COLS // HALF
    return first, min(COLS // HALF, SPEC - first)


def to_state(source, state, sem, first, count, begin):
    species, layers = pl.ds(first, count), pl.ds(begin, HALF)
    return pltpu.make_async_copy(
        source.reshape(SPEC, LAYERS, COLS).at[species, layers, :],
        state.reshape(SPEC, LAYERS, COLS).at[species, layers, :],
        sem,
    )


def first_kernel(
    tracers,
    wind,
    from_low,
    from_high,
    own_tend,
    other_tend,
    own,
    state,
    here,
    stack,
    sems,
):
    @pl.when(lax.axis_index("group") == 0)
    def _():
        def copy(layer):
            part = layer // HALF
            return to_state(here, state, sems.at[part], 0, SPEC, part * HALF)

        def after(layer):
            if layer % HALF == HALF - 1:
                copy(layer).start()

        advect(tracers, wind, from_low, from_high, own_tend, other_tend, here, after)
        for layer in (0, HALF):
            copy(layer).wait()

    @pl.when(lax.axis_index("group") == 1)
    def _():
        copies = [
            to_state(here, state, sems.at[piece], *slab(piece), HALF) for piece in range(PIECES)
        ]
        unpack(own, stack, here, HALF, lambda piece: copies[piece].start())
        for copy in copies:
            copy.wait()


def last_kernel(base, other, state, here, stack, sems):
    @pl.when(lax.axis_index("group") == 1)
    def _():
        copies = [
            to_state(here, state, sems.at[piece], *slab(piece), 0) for piece in range(PIECES)
        ]
        unpack(other, stack, here, 0, lambda piece: copies[piece].start())
        for copy in copies:
            copy.wait()


def cost(microseconds):
    return pl.CostEstimate(
        flops=int(microseconds * 1e9), bytes_accessed=int(microseconds * 2e6), transcendentals=0
    )


def bf16(*shape):
    return jax.ShapeDtypeStruct(shape, jnp.bfloat16)


def f32(*shape):
    return jax.ShapeDtypeStruct(shape, jnp.float32)


def local(
    species_amounts,
    air_warmth_kelvin,
    sunlight_strength,
    wind_stability_numbers,
    illuminated_marker,
    position_vertical_lookup,
    speed_constants,
    barrier_kelvins,
    consumed_species,
    outcome_species,
    outcome_fractions,
):
    amounts = species_amounts.reshape(ROWS, COLS)
    swap = [(0, 1), (1, 0)]
    swapped = lax.ppermute(amounts, "group", swap)

    table = jnp.concatenate(
        [
            consumed_species.astype(jnp.float32),
            outcome_species.astype(jnp.float32),
            outcome_fractions,
            speed_constants[None],
            barrier_kelvins[None],
        ]
    )
    weights, gather = pl.pallas_call(
        prepare_kernel,
        out_shape=(bf16(3 * SPAD, RPAD), bf16(RPAD, KDIM)),
        in_specs=[VMEM],
        out_specs=(VMEM, VMEM),
        scratch_shapes=[pltpu.VMEM((KDIM, RPAD), jnp.float32)],
        compiler_params=PARAMS,
        cost_estimate=cost(1),
        name="prepare",
    )(table)
    send, tendency = pl.pallas_call(
        chemistry_kernel,
        out_shape=(f32(PACKED, COLS), f32(HALF * SPAD, COLS)),
        in_specs=[VMEM] * 8,
        out_specs=(HBM, VMEM),
        scratch_shapes=[
            pltpu.VMEM((2 * KDIM, CELLS), jnp.bfloat16),
            pltpu.VMEM((SPAD, CELLS), jnp.float32),
            pltpu.VMEM((SPAD, CELLS), jnp.float32),
            pltpu.VMEM((PACKED, COLS), jnp.float32),
            pltpu.VMEM((3 * COLS, PACKED), jnp.bfloat16),
            pltpu.VMEM((PACKED, COLS), jnp.float32),
            pltpu.SemaphoreType.DMA((2,)),
        ],
        compiler_params=PARAMS,
        cost_estimate=cost(6),
        name="chemistry",
    )(
            amounts,
        swapped,
        illuminated_marker.reshape(COLS, COLS),
        position_vertical_lookup.reshape(COLS, COLS),
        air_warmth_kelvin,
        sunlight_strength,
        weights,
        gather,
    )
    received = lax.all_to_all(
        send.reshape(COLS, 1, PACKED),
        "tile",
        split_axis=0,
        concat_axis=0,
        axis_index_groups=[ORDER],
        tiled=True,
    )

    to_low, to_high = pl.pallas_call(
        edge_kernel,
        out_shape=(f32(EDGE * LAYERS, KDIM), f32(EDGE * LAYERS, KDIM)),
        in_specs=[VMEM, VMEM],
        out_specs=(VMEM, VMEM),
        scratch_shapes=[pltpu.VMEM((LAYERS, KDIM, COLS), jnp.float32)],
        compiler_params=PARAMS,
        cost_estimate=cost(1),
        name="edges",
    )(amounts, wind_stability_numbers)
    count = lax.axis_size("tile")
    both = ("group", "tile")
    from_low = lax.ppermute(to_high, both, [(i, i + 1) for i in range(count - 1)])
    from_high = lax.ppermute(to_low, both, [(i + 1, i) for i in range(count - 1)])
    other_tendency = lax.ppermute(tendency, "group", swap)
    received, other_tendency = lax.optimization_barrier((received, other_tendency))
    received = received.reshape(PACKED, COLS)
    other_received = lax.ppermute(received, "group", swap)
    base = pl.pallas_call(
        first_kernel,
        out_shape=f32(ROWS, COLS),
        in_specs=[VMEM] * 7,
        out_specs=HBM,
        scratch_shapes=[
            pltpu.VMEM((ROWS, COLS), jnp.float32),
            pltpu.VMEM((PACKED, COLS), jnp.float32),
            pltpu.SemaphoreType.DMA((PIECES,)),
        ],
        compiler_params=PARAMS,
        cost_estimate=cost(20),
        name="first",
    )(
            amounts,
        wind_stability_numbers,
        from_low,
        from_high,
        tendency,
        other_tendency,
        received,
    )
    state = pl.pallas_call(
        last_kernel,
        out_shape=f32(ROWS, COLS),
        in_specs=[HBM, VMEM],
        out_specs=HBM,
        input_output_aliases={0: 0},
        scratch_shapes=[
            pltpu.VMEM((ROWS, COLS), jnp.float32),
            pltpu.VMEM((PACKED, COLS), jnp.float32),
            pltpu.SemaphoreType.DMA((PIECES,)),
        ],
        compiler_params=PARAMS,
        cost_estimate=cost(1),
        name="last",
    )(base, other_received)
    return state.reshape(1, SPEC, LAYERS, COLS)


def solution(mesh):
    return jax.shard_map(
        local,
        mesh=mesh,
        in_specs=(
            P("group", None, None, "tile"),
            P(None, "tile"),
            P(None, "tile"),
            P(None, "tile"),
            P(),
            P(),
            P(),
            P(),
            P(),
            P(),
            P(),
        ),
        out_specs=P("group", None, None, "tile"),
        check_vma=False,
    )
```

time: 46.7 us -> 43.1 us (0.923)
  starting transfers between devices: 30 us -> 25 us
  waiting for transfers between devices: 6.47 us -> 8.64 us
  Pallas kernels: 8.5 us -> 7.01 us
  other arithmetic: 0.08 us -> 0.69 us
    all_to_all x1, waiting for transfers between devices: 0.43 us -> 7.92 us  [local(): lax.all_to_all(send.reshape(COLS, 1, PACKED), 'tile', split_axis=0, conca...]
    ppermute x2, starting transfers between devices: 6.91 us -> 1.33 us  [the longest x1 0.67 us: local(): lax.ppermute(to_high, both, [(i, i + 1) for i in range(count - 1)])]
    ppermute x2, waiting for transfers between devices: 4.49 us -> 0.01 us  [the longest x1 0.01 us: local(): lax.ppermute(to_high, both, [(i, i + 1) for i in range(count - 1)])]
    all_to_all x1, starting transfers between devices: 17.3 us -> 18.7 us  [local(): lax.all_to_all(send.reshape(COLS, 1, PACKED), 'tile', split_axis=0, conca...]
    ppermute x1, waiting for transfers between devices: 1.54 us -> 0.32 us  [local(): other_received = lax.ppermute(received, 'group', swap)]
    ppermute x1, starting transfers between devices: 1.84 us -> 1 us  [local(): other_received = lax.ppermute(received, 'group', swap)]
    pallas_call x3 -> x4, Pallas kernels: 7.43 us -> 6.61 us  [the longest x1 3.98 us: local(): pl.pallas_call(chemistry_kernel, out_shape=(f32(PACKED, COLS), f32(HALF *...]
    convert_element_type x0 -> x2, other arithmetic: none -> 0.69 us  [the longest x1 0.69 us: local(): consumed_species.astype(jnp.float32)]
  transfers between devices with their start and end apart: 6 -> 6, of which waited for: 3 -> 3; matrix products, arithmetic and copies ran while one was open for 0% -> 2% of each run, Pallas kernels for 3% -> 5%
where the time goes in v1:
time: 43.1 us; the launch traced here: 42.5 us
  starting transfers between devices  25 us (58%)
  waiting for transfers between devices  8.64 us (20%)
  Pallas kernels  7.01 us (16%)
  local copies, waits for them, and re-layouts  1.09 us (3%)
  other arithmetic  0.69 us (2%)
    all_to_all x1, starting transfers between devices, local(): lax.all_to_all(send.reshape(COLS, 1, PACKED), 'tile', split_axis=0, conca...  18.7 us
    all_to_all x1, waiting for transfers between devices, local(): lax.all_to_all(send.reshape(COLS, 1, PACKED), 'tile', split_axis=0, conca...  7.92 us
    pallas_call x1, Pallas kernels, local(): pl.pallas_call(chemistry_kernel, out_shape=(f32(PACKED, COLS), f32(HALF *...  3.98 us
    ppermute x1, starting transfers between devices, local(): swapped = lax.ppermute(amounts, 'group', swap)  3.24 us
    pallas_call x1, Pallas kernels, local(): pl.pallas_call(first_kernel, out_shape=f32(ROWS, COLS), in_specs=[VMEM] *...  1.11 us
    pallas_call x1, Pallas kernels, local(): pl.pallas_call(last_kernel, out_shape=f32(ROWS, COLS), in_specs=[HBM, VME...  1.11 us
    unnamed x20, local copies, waits for them, and re-layouts  1.06 us
    ppermute x1, starting transfers between devices, local(): other_received = lax.ppermute(received, 'group', swap)  1 us
  transfers between devices with their start and end apart: 6, of which 3 were waited for; matrix products, arithmetic and copies ran while one was open for 2% of the time, Pallas kernels for 5%

profile of v1, /device:TPU:1, one launch (start us, length us, event | category | flops | bytes accessed | tf_op | source)
XLA Modules:
  0.0 42.5 jit_solution(17023164615356850302)
XLA Ops:
  0.0 0.0 copy-start.6
  0.0 3.2 %collective-permute-start.2 = (f32[1760,128]{1,0:T(8,128)}, f32[1760,128]{1,0:T(8,128)S(1)}, u32[]{:S(2)}, u32[]{:S(2)}) collective-permute-start(f32[1760,128]{1,0:T(8,128)} %bitcast.10), channel_id=1, source_target_pairs={{0,128},{128,0},{1,129},{129,1},{2,130},{130,2},{3,131},{131,3},{4... | collective-permute-start | bytes 2703368 | tf_op jit(solution)/shard_map/ppermute | solution.py:405
  3.2 0.7 %convert_element_type.6 = f32[2,500]{1,0:T(2,128)S(1)} convert(s32[2,500]{1,0:T(2,128)} %param.19) | non-fusion elementwise | flops 1000 | bytes 8000 | tf_op jit(solution)/shard_map/convert_element_type | solution.py:409
  3.9 0.0 copy-done.6
  3.9 0.0 copy-start.7
  3.9 0.0 copy-start.9
  4.0 0.0 copy-start.8
  4.0 0.7 %copy-done.7 = f32[2,500]{1,0:T(2,128)S(1)} copy-done((f32[2,500]{1,0:T(2,128)S(1)}, f32[2,500]{1,0:T(2,128)}, u32[]{:S(2)}) %copy-start.7) | copy-done | bytes 4024
  4.6 0.0 copy-done.9
  4.6 0.0 copy-done.8
  4.7 0.0 copy-start
  4.7 0.0 copy-start.1
  4.7 0.0 copy-start.2
  4.7 0.0 copy-start.4
  4.7 0.4 prepare.1
  5.1 0.0 copy-start.3
  5.1 0.4 collective-permute-done.2.swapped
  5.5 0.3 copy-done
  5.9 0.0 copy-done.1
  5.9 0.0 copy-done.2
  5.9 0.0 copy-done.4
  5.9 0.0 copy-done.3
  5.9 4.0 %chemistry.1 = (f32[896,128]{1,0:T(8,128)}, f32[896,128]{1,0:T(8,128)S(1)}) custom-call(f32[1760,128]{1,0:T(8,128)S(1)} %bitcast.11, f32[1760,128]{1,0:T(8,128)S(1)} %collective-permute-done.2.swapped, s32[128,128]{1,0:T(8,128)S(1)} %bitcast.14, s32[128,128]{1,0:T(8,128)S(1)} %bitcast.15, f32[8,128]{1,0:T(8,128)S(1)} %copy-done.3, f32[8,128]{1,0:T(8,128)S(1)} %copy-done.4, ...), custom_call_target="tpu_custom_call" | custom-call | flops 6000000000 | bytes 12000000 | tf_op jit(solution)/shard_map/chemistry/pallas_call | solution.py:426
  9.9 0.0 copy-start.5
  9.9 18.7 %all-to-all-start = ((f32[128,1,896]{2,1,0:T(1,128)}), f32[128,1,896]{2,1,0:T(1,128)S(1)}, u32[]{:S(2)}, u32[]{:S(2)}) async-start(f32[128,1,896]{2,1,0:T(1,128)} %bitcast.5), calls=%async_computation | async-start | bytes 917504 | tf_op jit(solution)/shard_map/all_to_all | solution.py:453
  28.6 0.7 %collective-permute-start.3 = (f32[896,128]{1,0:T(8,128)S(1)}, f32[896,128]{1,0:T(8,128)S(1)}, u32[]{:S(2)}, u32[]{:S(2)}) collective-permute-start(f32[896,128]{1,0:T(8,128)S(1)} %get-tuple-element.17.own_tend), channel_id=1, source_target_pairs={{0,128},{128,0},{1,129},{129,1},{2,130},{130,2},{3,131},{131,3},{4... | collective-permute-start | bytes 1376264 | tf_op jit(solution)/shard_map/ppermute | solution.py:476
  29.3 0.0 copy-done.5
  29.3 0.4 edges.1
  29.7 0.7 %collective-permute-start = (f32[32,256]{1,0:T(8,128)S(1)}, f32[32,256]{1,0:T(8,128)S(1)}, u32[]{:S(2)}, u32[]{:S(2)}) collective-permute-start(f32[32,256]{1,0:T(8,128)S(1)} %get-tuple-element.13), channel_id=1, source_target_pairs={{0,1},{1,2},{2,3},{3,4},{4,5},{5,6},{6,7},{7,8},{8,9},{9,10},{10,1... | collective-permute-start | bytes 98312 | tf_op jit(solution)/shard_map/ppermute | solution.py:474
  30.4 0.7 %collective-permute-start.1 = (f32[32,256]{1,0:T(8,128)S(1)}, f32[32,256]{1,0:T(8,128)S(1)}, u32[]{:S(2)}, u32[]{:S(2)}) collective-permute-start(f32[32,256]{1,0:T(8,128)S(1)} %get-tuple-element.14), channel_id=1, source_target_pairs={{1,0},{2,1},{3,2},{4,3},{5,4},{6,5},{7,6},{8,7},{9,8},{10,9},{11,1... | collective-permute-start | bytes 98312 | tf_op jit(solution)/shard_map/ppermute | solution.py:475
  31.0 0.0 collective-permute-done.3.other_tend
  31.0 7.9 %all-to-all-done = f32[128,1,896]{2,1,0:T(1,128)S(1)} async-done(((f32[128,1,896]{2,1,0:T(1,128)}), f32[128,1,896]{2,1,0:T(1,128)S(1)}, u32[]{:S(2)}, u32[]{:S(2)}) %all-to-all-start) | async-done | bytes 458784 | tf_op jit(solution)/shard_map/all_to_all | solution.py:453
  39.0 1.0 %collective-permute-start.4 = (f32[896,128]{1,0:T(8,128)S(1)}, f32[896,128]{1,0:T(8,128)S(1)}, u32[]{:S(2)}, u32[]{:S(2)}) collective-permute-start(f32[896,128]{1,0:T(8,128)S(1)} %bitcast.8), channel_id=1, source_target_pairs={{0,128},{128,0},{1,129},{129,1},{2,130},{130,2},{3,131},{131,3},{4... | collective-permute-start | bytes 1376264 | tf_op jit(solution)/shard_map/ppermute | solution.py:479
  40.0 0.0 collective-permute-done.from_low
  40.0 0.0 collective-permute-done.1.from_high
  40.0 1.1 %first.1.base = f32[1760,128]{1,0:T(8,128)} custom-call(f32[1760,128]{1,0:T(8,128)S(1)} %bitcast.13, f32[8,128]{1,0:T(8,128)S(1)} %copy-done.5, f32[32,256]{1,0:T(8,128)S(1)} %collective-permute-done.from_low, f32[32,256]{1,0:T(8,128)S(1)} %collective-permute-done.1.from_high, f32[896,128]{1,0:T(8,128)S(1)} %get-tuple-element.17.own_tend, ...), custom_call_target="tpu_custom_call" | custom-call | flops 20000000000 | bytes 40000000 | tf_op jit(solution)/shard_map/first/pallas_call | solution.py:480
  41.1 0.3 collective-permute-done.4.other
  41.4 1.1 %last.1 = f32[1760,128]{1,0:T(8,128)} custom-call(f32[1760,128]{1,0:T(8,128)} %first.1.base, f32[896,128]{1,0:T(8,128)S(1)} %collective-permute-done.4.other), custom_call_target="tpu_custom_call", output_to_operand_aliasing={{}: (0, {})} | custom-call | flops 1000000000 | bytes 2000000 | tf_op jit(solution)/shard_map/last/pallas_call | solution.py:502
  (2 shorter events, 0.0 us)
Async XLA Ops:
  0.0 3.9 %copy-start.6 = (s32[2,500]{1,0:T(2,128)S(1)}, s32[2,500]{1,0:T(2,128)}, u32[]{:S(2)}) copy-start(s32[2,500]{1,0:T(2,128)} %param.20) | copy-start | bytes 12004
  0.0 5.5 %collective-permute-start.2 = (f32[1760,128]{1,0:T(8,128)}, f32[1760,128]{1,0:T(8,128)S(1)}, u32[]{:S(2)}, u32[]{:S(2)}) collective-permute-start(f32[1760,128]{1,0:T(8,128)} %bitcast.10), channel_id=1, source_target_pairs={{0,128},{128,0},{1,129},{129,1},{2,130},{130,2},{3,131},{131,3},{4... | collective-permute-start | bytes 2703368 | tf_op jit(solution)/shard_map/ppermute | solution.py:405
  3.9 0.7 %copy-start.7 = (f32[2,500]{1,0:T(2,128)S(1)}, f32[2,500]{1,0:T(2,128)}, u32[]{:S(2)}) copy-start(f32[2,500]{1,0:T(2,128)} %param.21) | copy-start | bytes 12004
  3.9 0.7 %copy-start.9 = (f32[500]{0:T(512)S(1)}, f32[500]{0:T(512)}, u32[]{:S(2)}) copy-start(f32[500]{0:T(512)} %param.18) | copy-start | bytes 6004
  4.0 0.7 %copy-start.8 = (f32[500]{0:T(512)S(1)}, f32[500]{0:T(512)}, u32[]{:S(2)}) copy-start(f32[500]{0:T(512)} %param.17) | copy-start | bytes 6004
  4.7 1.2 %copy-start = (f32[1,220,8,128]{3,2,1,0:T(8,128)S(1)}, f32[1,220,8,128]{3,2,1,0:T(8,128)}, u32[]{:S(2)}) copy-start(f32[1,220,8,128]{3,2,1,0:T(8,128)} %param.11) | copy-start | bytes 2703364
  4.7 1.2 %copy-start.1 = (s32[16384]{0:T(1024)S(1)}, s32[16384]{0:T(1024)}, u32[]{:S(2)}) copy-start(s32[16384]{0:T(1024)} %param.15) | copy-start | bytes 196612
  4.7 1.2 %copy-start.2 = (s32[16384]{0:T(1024)S(1)}, s32[16384]{0:T(1024)}, u32[]{:S(2)}) copy-start(s32[16384]{0:T(1024)} %param.16) | copy-start | bytes 196612
  4.7 1.1 %copy-start.4 = (f32[8,128]{1,0:T(8,128)S(1)}, f32[8,128]{1,0:T(8,128)}, u32[]{:S(2)}) copy-start(f32[8,128]{1,0:T(8,128)} %light.1) | copy-start | bytes 12292
  5.1 0.8 %copy-start.3 = (f32[8,128]{1,0:T(8,128)S(1)}, f32[8,128]{1,0:T(8,128)}, u32[]{:S(2)}) copy-start(f32[8,128]{1,0:T(8,128)} %heat.1) | copy-start | bytes 12292
  9.9 19.4 %copy-start.5 = (f32[8,128]{1,0:T(8,128)S(1)}, f32[8,128]{1,0:T(8,128)}, u32[]{:S(2)}) copy-start(f32[8,128]{1,0:T(8,128)} %wind.3) | copy-start | bytes 12292
  9.9 29.1 %all-to-all-start = ((f32[128,1,896]{2,1,0:T(1,128)}), f32[128,1,896]{2,1,0:T(1,128)S(1)}, u32[]{:S(2)}, u32[]{:S(2)}) async-start(f32[128,1,896]{2,1,0:T(1,128)} %bitcast.5), calls=%async_computation | async-start | bytes 917504 | tf_op jit(solution)/shard_map/all_to_all | solution.py:453
  28.6 2.5 %collective-permute-start.3 = (f32[896,128]{1,0:T(8,128)S(1)}, f32[896,128]{1,0:T(8,128)S(1)}, u32[]{:S(2)}, u32[]{:S(2)}) collective-permute-start(f32[896,128]{1,0:T(8,128)S(1)} %get-tuple-element.17.own_tend), channel_id=1, source_target_pairs={{0,128},{128,0},{1,129},{129,1},{2,130},{130,2},{3,131},{131,3},{4... | collective-permute-start | bytes 1376264 | tf_op jit(solution)/shard_map/ppermute | solution.py:476
  29.7 10.3 %collective-permute-start = (f32[32,256]{1,0:T(8,128)S(1)}, f32[32,256]{1,0:T(8,128)S(1)}, u32[]{:S(2)}, u32[]{:S(2)}) collective-permute-start(f32[32,256]{1,0:T(8,128)S(1)} %get-tuple-element.13), channel_id=1, source_target_pairs={{0,1},{1,2},{2,3},{3,4},{4,5},{5,6},{6,7},{7,8},{8,9},{9,10},{10,1... | collective-permute-start | bytes 98312 | tf_op jit(solution)/shard_map/ppermute | solution.py:474
  30.4 9.6 %collective-permute-start.1 = (f32[32,256]{1,0:T(8,128)S(1)}, f32[32,256]{1,0:T(8,128)S(1)}, u32[]{:S(2)}, u32[]{:S(2)}) collective-permute-start(f32[32,256]{1,0:T(8,128)S(1)} %get-tuple-element.14), channel_id=1, source_target_pairs={{1,0},{2,1},{3,2},{4,3},{5,4},{6,5},{7,6},{8,7},{9,8},{10,9},{11,1... | collective-permute-start | bytes 98312 | tf_op jit(solution)/shard_map/ppermute | solution.py:475
  39.0 2.4 %collective-permute-start.4 = (f32[896,128]{1,0:T(8,128)S(1)}, f32[896,128]{1,0:T(8,128)S(1)}, u32[]{:S(2)}, u32[]{:S(2)}) collective-permute-start(f32[896,128]{1,0:T(8,128)S(1)} %bitcast.8), channel_id=1, source_target_pairs={{0,128},{128,0},{1,129},{129,1},{2,130},{130,2},{3,131},{131,3},{4... | collective-permute-start | bytes 1376264 | tf_op jit(solution)/shard_map/ppermute | solution.py:479

commit v2 on v1

--- a/solution.py
+++ b/solution.py
@@ -22,12 +22,15 @@
 CELLS = HALF * COLS
 PIECES = 7
 PACKED = PIECES * COLS
+PARTS = 2
+SENDS = 4
 CHUNK = 256
 EDGE = 4
 DARK = -1024.0
 
-MIDDLE = (4, 5, 3, 6, 2, 7, 1, 0)
-ORDER = [z * 16 + x * 4 + y for y in range(3, -1, -1) for x in range(3, -1, -1) for z in MIDDLE]
+MIDDLE = (4, 3, 5, 2, 6, 1, 7, 0)
+INNER = (2, 1, 3, 0)
+ORDER = [z * 16 + x * 4 + y for y in INNER for x in INNER for z in MIDDLE]
 
 VMEM = pl.BlockSpec(memory_space=pltpu.VMEM)
 HBM = pl.BlockSpec(memory_space=pltpu.HBM)
@@ -43,20 +46,21 @@
     return jnp.dot(a, b, preferred_element_type=jnp.float32)
 
 
+def pick(table, index):
+    out = jnp.zeros_like(index)
+    for at, value in enumerate(table):
+        out = jnp.where(index == at, value, out)
+    return out
+
+
 def tile_at(place):
-    step = place % 8
-    z = jnp.zeros_like(place)
-    for at, value in enumerate(MIDDLE):
-        z = jnp.where(step == at, value, z)
-    return z * 16 + (3 - place // 8 % 4) * 4 + 3 - place // 32
+    return pick(MIDDLE, place % 8) * 16 + pick(INNER, place // 8 % 4) * 4 + pick(INNER, place // 32)
 
 
 def place_of(tile):
-    z = tile // 16
-    step = jnp.zeros_like(tile)
-    for at, value in enumerate(MIDDLE):
-        step = jnp.where(z == value, at, step)
-    return (3 - tile % 4) * 32 + (3 - tile // 4 % 4) * 8 + step
+    middle = [MIDDLE.index(z) for z in range(8)]
+    inner = [INNER.index(z) for z in range(4)]
+    return pick(inner, tile % 4) * 32 + pick(inner, tile // 4 % 4) * 8 + pick(middle, tile // 16)
 
 
 def prepare_kernel(table, weights, gather, turning):
@@ -146,8 +150,7 @@
     now[...] = start[...]
     chunks = [pl.ds(at, CHUNK) for at in range(0, CELLS, CHUNK)]
 
-    @pl.loop(0, sweeps)
-    def _(_):
+    def sweep():
         for cells in chunks:
             log_high, log_low = high_low(lax.log2(now[:, cells]))
             logs[0:SPAD, cells] = log_high
@@ -162,34 +165,40 @@
             concen = now[:, cells]
             now[:, cells] = concen * (start[:, cells] + gain) / (concen + both[:SPAD])
 
+    @pl.loop(0, sweeps // 2)
+    def _(_):
+        sweep()
+        sweep()
+
     lane = lax.broadcasted_iota(jnp.int32, (COLS, COLS), 1)
     column = jnp.sum(jnp.where(lane == tile, lookup[...], 0), axis=1, keepdims=True)
-    pick = jnp.where(lane == column - tile * COLS, 1.0, 0.0)
+    chosen = jnp.where(lane == column - tile * COLS, 1.0, 0.0)
     ordered = jnp.where(lane == tile_at(lax.broadcasted_iota(jnp.int32, (COLS, COLS), 0)), 1.0, 0.0)
-    choose = dot(ordered.astype(jnp.bfloat16), pick.astype(jnp.bfloat16)).astype(jnp.bfloat16)
+    choose = dot(ordered.astype(jnp.bfloat16), chosen.astype(jnp.bfloat16)).astype(jnp.bfloat16)
     for layer in range(HALF):
         cells = pl.ds(layer * COLS, COLS)
         stack[pl.ds(layer, SPEC, stride=HALF), :] = now[0:SPEC, cells]
     stack[HALF * SPEC :, :] = jnp.zeros((PACKED - HALF * SPEC, COLS), jnp.float32)
     for piece in range(PIECES):
         rest = jnp.transpose(stack[pl.ds(piece * COLS, COLS), :])
-        for part in range(3):
+        for part in range(PARTS):
             rounded = rest.astype(jnp.bfloat16)
             rest = rest - rounded.astype(jnp.float32)
             parts[pl.ds(part * COLS, COLS), pl.ds(piece * COLS, COLS)] = rounded
     copies = []
-    for half in range(2):
-        owners = COLS // 2
+    owners = COLS // SENDS
+    for part in range(SENDS):
         turned = dot(
-            jnp.concatenate([choose[half * owners : (half + 1) * owners]] * 3, axis=1), parts[...]
+            jnp.concatenate([choose[part * owners : (part + 1) * owners]] * PARTS, axis=1),
+            parts[...],
         )
         for piece in range(PIECES):
-            packed[pl.ds(half * owners * PIECES + piece, owners, stride=PIECES), :] = turned[
+            packed[pl.ds(part * owners * PIECES + piece, owners, stride=PIECES), :] = turned[
                 :, piece * COLS : (piece + 1) * COLS
             ]
-        rows = pl.ds(half * owners * PIECES, owners * PIECES)
-        copies.append(pltpu.make_async_copy(packed.at[rows], send.at[rows], sems.at[half]))
-        copies[half].start()
+        rows = pl.ds(part * owners * PIECES, owners * PIECES)
+        copies.append(pltpu.make_async_copy(packed.at[rows], send.at[rows], sems.at[part]))
+        copies[part].start()
     for layer in range(HALF):
         cells = pl.ds(layer * COLS, COLS)
         tendency[pl.ds(layer * SPAD, SPAD), :] = now[:, cells] - start[:, cells]
@@ -201,30 +210,33 @@
     return lax.dot_general(a, b, (((1,), (1,)), ((), ())), preferred_element_type=jnp.float32)
 
 
-def edge_kernel(tracers, wind, to_low, to_high, padded):
+def edge_kernel(tracers, wind, far, near, padded):
+    odd = lax.axis_index("tile") % 2 == 1
     row = lax.broadcasted_iota(jnp.int32, (2 * EDGE, COLS), 0)
     column = lax.broadcasted_iota(jnp.int32, (2 * EDGE, COLS), 1)
-    pick = jnp.where(column == (row + COLS - EDGE) % COLS, 1.0, 0.0).astype(jnp.bfloat16)
+    choose = jnp.where(column == (row + COLS - EDGE) % COLS, 1.0, 0.0).astype(jnp.bfloat16)
     for layer in range(LAYERS):
         padded[layer, SPEC - 4 :, :] = jnp.zeros((KDIM - SPEC + 4, COLS), jnp.float32)
         padded[layer, 0:SPEC, :] = tracers[pl.ds(layer, SPEC, stride=LAYERS), :]
         padded[layer, SPEC : SPEC + 1, :] = wind[layer : layer + 1, :]
     for layer in range(LAYERS):
         high, low = high_low(padded[layer])
-        picked = across(pick, high) + across(pick, low)
-        to_high[pl.ds(layer * EDGE, EDGE), :] = picked[:EDGE]
-        to_low[pl.ds(layer * EDGE, EDGE), :] = picked[EDGE:]
-
-
-def advect(tracers, wind, from_low, from_high, own_tend, other_tend, state, after):
+        picked = across(choose, high) + across(choose, low)
+        to_high, to_low = picked[:EDGE], picked[EDGE:]
+        far[pl.ds(layer * EDGE, EDGE), :] = jnp.where(odd, to_high, to_low)
+        near[pl.ds(layer * EDGE, EDGE), :] = jnp.where(odd, to_low, to_high)
+
+
+def advect(tracers, wind, far, near, own_tend, other_tend, state, after):
     tile = lax.axis_index("tile")
+    odd = tile % 2 == 1
     side = EDGE * LAYERS
     low_there = jnp.where(tile > 0, 1.0, 0.0)
     high_there = jnp.where(tile < COLS - 1, 1.0, 0.0)
     beside = jnp.concatenate(
         [
-            from_low[...] * low_there,
-            from_high[...] * high_there,
+            jnp.where(odd, near[...], far[...]) * low_there,
+            jnp.where(odd, far[...], near[...]) * high_there,
             jnp.zeros((COLS - 2 * side, KDIM), jnp.float32),
         ],
         axis=0,
@@ -328,8 +340,8 @@
 def first_kernel(
     tracers,
     wind,
-    from_low,
-    from_high,
+    far,
+    near,
     own_tend,
     other_tend,
     own,
@@ -348,7 +360,7 @@
             if layer % HALF == HALF - 1:
                 copy(layer).start()
 
-        advect(tracers, wind, from_low, from_high, own_tend, other_tend, here, after)
+        advect(tracers, wind, far, near, own_tend, other_tend, here, after)
         for layer in (0, HALF):
             copy(layer).wait()
 
@@ -385,6 +397,10 @@
 
 def f32(*shape):
     return jax.ShapeDtypeStruct(shape, jnp.float32)
+
+
+def exchanged(tiles):
+    return [pair for i in tiles for pair in ((i, i + 1), (i + 1, i))]
 
 
 def local(
@@ -433,9 +449,9 @@
             pltpu.VMEM((SPAD, CELLS), jnp.float32),
             pltpu.VMEM((SPAD, CELLS), jnp.float32),
             pltpu.VMEM((PACKED, COLS), jnp.float32),
-            pltpu.VMEM((3 * COLS, PACKED), jnp.bfloat16),
+            pltpu.VMEM((PARTS * COLS, PACKED), jnp.bfloat16),
             pltpu.VMEM((PACKED, COLS), jnp.float32),
-            pltpu.SemaphoreType.DMA((2,)),
+            pltpu.SemaphoreType.DMA((SENDS,)),
         ],
         compiler_params=PARAMS,
         cost_estimate=cost(6),
@@ -459,7 +475,7 @@
         tiled=True,
     )
 
-    to_low, to_high = pl.pallas_call(
+    far, near = pl.pallas_call(
         edge_kernel,
         out_shape=(f32(EDGE * LAYERS, KDIM), f32(EDGE * LAYERS, KDIM)),
         in_specs=[VMEM, VMEM],
@@ -471,8 +487,8 @@
     )(amounts, wind_stability_numbers)
     count = lax.axis_size("tile")
     both = ("group", "tile")
-    from_low = lax.ppermute(to_high, both, [(i, i + 1) for i in range(count - 1)])
-    from_high = lax.ppermute(to_low, both, [(i + 1, i) for i in range(count - 1)])
+    far = lax.ppermute(far, both, exchanged(range(1, count - 1, 2)))
+    near = lax.ppermute(near, both, exchanged(range(0, count, 2)))
     other_tendency = lax.ppermute(tendency, "group", swap)
     received, other_tendency = lax.optimization_barrier((received, other_tendency))
     received = received.reshape(PACKED, COLS)
@@ -493,8 +509,8 @@
     )(
             amounts,
         wind_stability_numbers,
-        from_low,
-        from_high,
+        far,
+        near,
         tendency,
         other_tendency,
         received,

time: 43.1 us -> 42.5 us (0.986)
  Pallas kernels: 7.01 us -> 9.33 us
  starting transfers between devices: 25 us -> 22.7 us
    pallas_call x1, Pallas kernels: 3.98 us -> 6.3 us  [local(): pl.pallas_call(chemistry_kernel, out_shape=(f32(PACKED, COLS), f32(HALF *...]
    all_to_all x1, starting transfers between devices: 18.7 us -> 16.6 us  [local(): lax.all_to_all(send.reshape(COLS, 1, PACKED), 'tile', split_axis=0, conca...]
where the time goes in v2:
time: 42.5 us; the launch traced here: 42.3 us
  starting transfers between devices  22.7 us (53%)
  Pallas kernels  9.33 us (22%)
  waiting for transfers between devices  8.39 us (20%)
  local copies, waits for them, and re-layouts  1.09 us (3%)
  other arithmetic  0.69 us (2%)
    all_to_all x1, starting transfers between devices, local(): lax.all_to_all(send.reshape(COLS, 1, PACKED), 'tile', split_axis=0, conca...  16.6 us
    all_to_all x1, waiting for transfers between devices, local(): lax.all_to_all(send.reshape(COLS, 1, PACKED), 'tile', split_axis=0, conca...  7.67 us
    pallas_call x1, Pallas kernels, local(): pl.pallas_call(chemistry_kernel, out_shape=(f32(PACKED, COLS), f32(HALF *...  6.3 us
    ppermute x1, starting transfers between devices, local(): swapped = lax.ppermute(amounts, 'group', swap)  3.24 us
    pallas_call x1, Pallas kernels, local(): pl.pallas_call(first_kernel, out_shape=f32(ROWS, COLS), in_specs=[VMEM] *...  1.11 us
    pallas_call x1, Pallas kernels, local(): pl.pallas_call(last_kernel, out_shape=f32(ROWS, COLS), in_specs=[HBM, VME...  1.11 us
    unnamed x20, local copies, waits for them, and re-layouts  1.06 us
  transfers between devices with their start and end apart: 6, of which 3 were waited for; matrix products, arithmetic and copies ran while one was open for 2% of the time, Pallas kernels for 5%

profile of v2, /device:TPU:1, one launch (start us, length us, event | category | flops | bytes accessed | tf_op | source)
XLA Modules:
  0.0 42.3 jit_solution(5043402533216480547)
XLA Ops:
  0.0 0.0 copy-start.6
  0.0 3.2 %collective-permute-start.2 = (f32[1760,128]{1,0:T(8,128)}, f32[1760,128]{1,0:T(8,128)S(1)}, u32[]{:S(2)}, u32[]{:S(2)}) collective-permute-start(f32[1760,128]{1,0:T(8,128)} %bitcast.10), channel_id=1, source_target_pairs={{0,128},{128,0},{1,129},{129,1},{2,130},{130,2},{3,131},{131,3},{4... | collective-permute-start | bytes 2703368 | tf_op jit(solution)/shard_map/ppermute | solution.py:421
  3.2 0.7 %convert_element_type.6 = f32[2,500]{1,0:T(2,128)S(1)} convert(s32[2,500]{1,0:T(2,128)} %param.19) | non-fusion elementwise | flops 1000 | bytes 8000 | tf_op jit(solution)/shard_map/convert_element_type | solution.py:425
  3.9 0.0 copy-done.6
  3.9 0.0 copy-start.7
  3.9 0.0 copy-start.9
  4.0 0.0 copy-start.8
  4.0 0.7 %copy-done.7 = f32[2,500]{1,0:T(2,128)S(1)} copy-done((f32[2,500]{1,0:T(2,128)S(1)}, f32[2,500]{1,0:T(2,128)}, u32[]{:S(2)}) %copy-start.7) | copy-done | bytes 4024
  4.6 0.0 copy-done.9
  4.6 0.0 copy-done.8
  4.7 0.0 copy-start
  4.7 0.0 copy-start.1
  4.7 0.0 copy-start.2
  4.7 0.0 copy-start.4
  4.7 0.4 prepare.1
  5.1 0.0 copy-start.3
  5.1 0.4 collective-permute-done.2.swapped
  5.5 0.3 copy-done
  5.9 0.0 copy-done.1
  5.9 0.0 copy-done.2
  5.9 0.0 copy-done.4
  5.9 0.0 copy-done.3
  5.9 6.3 %chemistry.1 = (f32[896,128]{1,0:T(8,128)}, f32[896,128]{1,0:T(8,128)S(1)}) custom-call(f32[1760,128]{1,0:T(8,128)S(1)} %bitcast.11, f32[1760,128]{1,0:T(8,128)S(1)} %collective-permute-done.2.swapped, s32[128,128]{1,0:T(8,128)S(1)} %bitcast.14, s32[128,128]{1,0:T(8,128)S(1)} %bitcast.15, f32[8,128]{1,0:T(8,128)S(1)} %copy-done.3, f32[8,128]{1,0:T(8,128)S(1)} %copy-done.4, ...), custom_call_target="tpu_custom_call" | custom-call | flops 6000000000 | bytes 12000000 | tf_op jit(solution)/shard_map/chemistry/pallas_call | solution.py:442
  12.2 0.0 copy-start.5
  12.2 16.6 %all-to-all-start = ((f32[128,1,896]{2,1,0:T(1,128)}), f32[128,1,896]{2,1,0:T(1,128)S(1)}, u32[]{:S(2)}, u32[]{:S(2)}) async-start(f32[128,1,896]{2,1,0:T(1,128)} %bitcast.5), calls=%async_computation | async-start | bytes 917504 | tf_op jit(solution)/shard_map/all_to_all | solution.py:469
  28.8 0.7 %collective-permute-start.3 = (f32[896,128]{1,0:T(8,128)S(1)}, f32[896,128]{1,0:T(8,128)S(1)}, u32[]{:S(2)}, u32[]{:S(2)}) collective-permute-start(f32[896,128]{1,0:T(8,128)S(1)} %get-tuple-element.17.own_tend), channel_id=1, source_target_pairs={{0,128},{128,0},{1,129},{129,1},{2,130},{130,2},{3,131},{131,3},{4... | collective-permute-start | bytes 1376264 | tf_op jit(solution)/shard_map/ppermute | solution.py:492
  29.5 0.0 copy-done.5
  29.6 0.4 edges.1
  30.0 0.7 %collective-permute-start = (f32[32,256]{1,0:T(8,128)S(1)}, f32[32,256]{1,0:T(8,128)S(1)}, u32[]{:S(2)}, u32[]{:S(2)}) collective-permute-start(f32[32,256]{1,0:T(8,128)S(1)} %get-tuple-element.13), channel_id=1, source_target_pairs={{1,2},{2,1},{3,4},{4,3},{5,6},{6,5},{7,8},{8,7},{9,10},{10,9},{11,... | collective-permute-start | bytes 98312 | tf_op jit(solution)/shard_map/ppermute | solution.py:490
  30.6 0.7 %collective-permute-start.1 = (f32[32,256]{1,0:T(8,128)S(1)}, f32[32,256]{1,0:T(8,128)S(1)}, u32[]{:S(2)}, u32[]{:S(2)}) collective-permute-start(f32[32,256]{1,0:T(8,128)S(1)} %get-tuple-element.14), channel_id=1, source_target_pairs={{0,1},{1,0},{2,3},{3,2},{4,5},{5,4},{6,7},{7,6},{8,9},{9,8},{10,11... | collective-permute-start | bytes 98312 | tf_op jit(solution)/shard_map/ppermute | solution.py:491
  31.3 0.0 collective-permute-done.3.other_tend
  31.3 7.7 %all-to-all-done = f32[128,1,896]{2,1,0:T(1,128)S(1)} async-done(((f32[128,1,896]{2,1,0:T(1,128)}), f32[128,1,896]{2,1,0:T(1,128)S(1)}, u32[]{:S(2)}, u32[]{:S(2)}) %all-to-all-start) | async-done | bytes 458784 | tf_op jit(solution)/shard_map/all_to_all | solution.py:469
  39.0 0.8 %collective-permute-start.4 = (f32[896,128]{1,0:T(8,128)S(1)}, f32[896,128]{1,0:T(8,128)S(1)}, u32[]{:S(2)}, u32[]{:S(2)}) collective-permute-start(f32[896,128]{1,0:T(8,128)S(1)} %bitcast.8), channel_id=1, source_target_pairs={{0,128},{128,0},{1,129},{129,1},{2,130},{130,2},{3,131},{131,3},{4... | collective-permute-start | bytes 1376264 | tf_op jit(solution)/shard_map/ppermute | solution.py:495
  39.8 0.0 collective-permute-done.far
  39.8 0.0 collective-permute-done.1.near
  39.8 1.1 %first.1.base = f32[1760,128]{1,0:T(8,128)} custom-call(f32[1760,128]{1,0:T(8,128)S(1)} %bitcast.13, f32[8,128]{1,0:T(8,128)S(1)} %copy-done.5, f32[32,256]{1,0:T(8,128)S(1)} %collective-permute-done.far, f32[32,256]{1,0:T(8,128)S(1)} %collective-permute-done.1.near, f32[896,128]{1,0:T(8,128)S(1)} %get-tuple-element.17.own_tend, ...), custom_call_target="tpu_custom_call" | custom-call | flops 20000000000 | bytes 40000000 | tf_op jit(solution)/shard_map/first/pallas_call | solution.py:496
  40.9 0.3 collective-permute-done.4.other
  41.2 1.1 %last.1 = f32[1760,128]{1,0:T(8,128)} custom-call(f32[1760,128]{1,0:T(8,128)} %first.1.base, f32[896,128]{1,0:T(8,128)S(1)} %collective-permute-done.4.other), custom_call_target="tpu_custom_call", output_to_operand_aliasing={{}: (0, {})} | custom-call | flops 1000000000 | bytes 2000000 | tf_op jit(solution)/shard_map/last/pallas_call | solution.py:518
  (2 shorter events, 0.0 us)
Async XLA Ops:
  0.0 3.9 %copy-start.6 = (s32[2,500]{1,0:T(2,128)S(1)}, s32[2,500]{1,0:T(2,128)}, u32[]{:S(2)}) copy-start(s32[2,500]{1,0:T(2,128)} %param.20) | copy-start | bytes 12004
  0.0 5.5 %collective-permute-start.2 = (f32[1760,128]{1,0:T(8,128)}, f32[1760,128]{1,0:T(8,128)S(1)}, u32[]{:S(2)}, u32[]{:S(2)}) collective-permute-start(f32[1760,128]{1,0:T(8,128)} %bitcast.10), channel_id=1, source_target_pairs={{0,128},{128,0},{1,129},{129,1},{2,130},{130,2},{3,131},{131,3},{4... | collective-permute-start | bytes 2703368 | tf_op jit(solution)/shard_map/ppermute | solution.py:421
  3.9 0.7 %copy-start.7 = (f32[2,500]{1,0:T(2,128)S(1)}, f32[2,500]{1,0:T(2,128)}, u32[]{:S(2)}) copy-start(f32[2,500]{1,0:T(2,128)} %param.21) | copy-start | bytes 12004
  3.9 0.7 %copy-start.9 = (f32[500]{0:T(512)S(1)}, f32[500]{0:T(512)}, u32[]{:S(2)}) copy-start(f32[500]{0:T(512)} %param.18) | copy-start | bytes 6004
  4.0 0.7 %copy-start.8 = (f32[500]{0:T(512)S(1)}, f32[500]{0:T(512)}, u32[]{:S(2)}) copy-start(f32[500]{0:T(512)} %param.17) | copy-start | bytes 6004
  4.7 1.2 %copy-start = (f32[1,220,8,128]{3,2,1,0:T(8,128)S(1)}, f32[1,220,8,128]{3,2,1,0:T(8,128)}, u32[]{:S(2)}) copy-start(f32[1,220,8,128]{3,2,1,0:T(8,128)} %param.11) | copy-start | bytes 2703364
  4.7 1.2 %copy-start.1 = (s32[16384]{0:T(1024)S(1)}, s32[16384]{0:T(1024)}, u32[]{:S(2)}) copy-start(s32[16384]{0:T(1024)} %param.15) | copy-start | bytes 196612
  4.7 1.2 %copy-start.2 = (s32[16384]{0:T(1024)S(1)}, s32[16384]{0:T(1024)}, u32[]{:S(2)}) copy-start(s32[16384]{0:T(1024)} %param.16) | copy-start | bytes 196612
  4.7 1.1 %copy-start.4 = (f32[8,128]{1,0:T(8,128)S(1)}, f32[8,128]{1,0:T(8,128)}, u32[]{:S(2)}) copy-start(f32[8,128]{1,0:T(8,128)} %light.1) | copy-start | bytes 12292
  5.1 0.8 %copy-start.3 = (f32[8,128]{1,0:T(8,128)S(1)}, f32[8,128]{1,0:T(8,128)}, u32[]{:S(2)}) copy-start(f32[8,128]{1,0:T(8,128)} %heat.1) | copy-start | bytes 12292
  12.2 17.4 %copy-start.5 = (f32[8,128]{1,0:T(8,128)S(1)}, f32[8,128]{1,0:T(8,128)}, u32[]{:S(2)}) copy-start(f32[8,128]{1,0:T(8,128)} %wind.3) | copy-start | bytes 12292
  12.2 26.8 %all-to-all-start = ((f32[128,1,896]{2,1,0:T(1,128)}), f32[128,1,896]{2,1,0:T(1,128)S(1)}, u32[]{:S(2)}, u32[]{:S(2)}) async-start(f32[128,1,896]{2,1,0:T(1,128)} %bitcast.5), calls=%async_computation | async-start | bytes 917504 | tf_op jit(solution)/shard_map/all_to_all | solution.py:469
  28.8 2.5 %collective-permute-start.3 = (f32[896,128]{1,0:T(8,128)S(1)}, f32[896,128]{1,0:T(8,128)S(1)}, u32[]{:S(2)}, u32[]{:S(2)}) collective-permute-start(f32[896,128]{1,0:T(8,128)S(1)} %get-tuple-element.17.own_tend), channel_id=1, source_target_pairs={{0,128},{128,0},{1,129},{129,1},{2,130},{130,2},{3,131},{131,3},{4... | collective-permute-start | bytes 1376264 | tf_op jit(solution)/shard_map/ppermute | solution.py:492
  30.0 9.8 %collective-permute-start = (f32[32,256]{1,0:T(8,128)S(1)}, f32[32,256]{1,0:T(8,128)S(1)}, u32[]{:S(2)}, u32[]{:S(2)}) collective-permute-start(f32[32,256]{1,0:T(8,128)S(1)} %get-tuple-element.13), channel_id=1, source_target_pairs={{1,2},{2,1},{3,4},{4,3},{5,6},{6,5},{7,8},{8,7},{9,10},{10,9},{11,... | collective-permute-start | bytes 98312 | tf_op jit(solution)/shard_map/ppermute | solution.py:490
  30.6 9.1 %collective-permute-start.1 = (f32[32,256]{1,0:T(8,128)S(1)}, f32[32,256]{1,0:T(8,128)S(1)}, u32[]{:S(2)}, u32[]{:S(2)}) collective-permute-start(f32[32,256]{1,0:T(8,128)S(1)} %get-tuple-element.14), channel_id=1, source_target_pairs={{0,1},{1,0},{2,3},{3,2},{4,5},{5,4},{6,7},{7,6},{8,9},{9,8},{10,11... | collective-permute-start | bytes 98312 | tf_op jit(solution)/shard_map/ppermute | solution.py:491
  39.0 2.2 %collective-permute-start.4 = (f32[896,128]{1,0:T(8,128)S(1)}, f32[896,128]{1,0:T(8,128)S(1)}, u32[]{:S(2)}, u32[]{:S(2)}) collective-permute-start(f32[896,128]{1,0:T(8,128)S(1)} %bitcast.8), channel_id=1, source_target_pairs={{0,128},{128,0},{1,129},{129,1},{2,130},{130,2},{3,131},{131,3},{4... | collective-permute-start | bytes 1376264 | tf_op jit(solution)/shard_map/ppermute | solution.py:495

commit v3 on v2

--- a/solution.py
+++ b/solution.py
@@ -23,14 +23,14 @@
 PIECES = 7
 PACKED = PIECES * COLS
 PARTS = 2
-SENDS = 4
+SENDS = 1
 CHUNK = 256
 EDGE = 4
 DARK = -1024.0
 
 MIDDLE = (4, 3, 5, 2, 6, 1, 7, 0)
 INNER = (2, 1, 3, 0)
-ORDER = [z * 16 + x * 4 + y for y in INNER for x in INNER for z in MIDDLE]
+ORDER = [z * 16 + x * 4 + y for z in MIDDLE for x in INNER for y in INNER]
 
 VMEM = pl.BlockSpec(memory_space=pltpu.VMEM)
 HBM = pl.BlockSpec(memory_space=pltpu.HBM)
@@ -54,13 +54,13 @@
 
 
 def tile_at(place):
-    return pick(MIDDLE, place % 8) * 16 + pick(INNER, place // 8 % 4) * 4 + pick(INNER, place // 32)
+    return pick(MIDDLE, place // 16) * 16 + pick(INNER, place // 4 % 4) * 4 + pick(INNER, place % 4)
 
 
 def place_of(tile):
     middle = [MIDDLE.index(z) for z in range(8)]
     inner = [INNER.index(z) for z in range(4)]
-    return pick(inner, tile % 4) * 32 + pick(inner, tile // 4 % 4) * 8 + pick(middle, tile // 16)
+    return pick(middle, tile // 16) * 16 + pick(inner, tile // 4 % 4) * 4 + pick(inner, tile % 4)
 
 
 def prepare_kernel(table, weights, gather, turning):

time: 42.5 us -> 41.4 us (0.974); the launches traced: 42.3 us -> 42 us
  waiting for transfers between devices: 8.39 us -> 7.43 us
  starting transfers between devices: 22.7 us -> 23.4 us
    all_to_all x1, waiting for transfers between devices: 7.67 us -> 6.71 us  [local(): lax.all_to_all(send.reshape(COLS, 1, PACKED), 'tile', split_axis=0, conca...]
    ppermute x1, starting transfers between devices: 0.78 us -> 1.5 us  [local(): other_received = lax.ppermute(received, 'group', swap)]
where the time goes in v3:
time: 41.4 us; the launch traced here: 42 us
  starting transfers between devices  23.4 us (57%)
  Pallas kernels  9.25 us (22%)
  waiting for transfers between devices  7.43 us (18%)
  local copies, waits for them, and re-layouts  1.09 us (3%)
  other arithmetic  0.69 us (2%)
    all_to_all x1, starting transfers between devices, local(): lax.all_to_all(send.reshape(COLS, 1, PACKED), 'tile', split_axis=0, conca...  16.6 us
    all_to_all x1, waiting for transfers between devices, local(): lax.all_to_all(send.reshape(COLS, 1, PACKED), 'tile', split_axis=0, conca...  6.71 us
    pallas_call x1, Pallas kernels, local(): pl.pallas_call(chemistry_kernel, out_shape=(f32(PACKED, COLS), f32(HALF *...  6.22 us
    ppermute x1, starting transfers between devices, local(): swapped = lax.ppermute(amounts, 'group', swap)  3.24 us
    ppermute x1, starting transfers between devices, local(): other_received = lax.ppermute(received, 'group', swap)  1.5 us
    pallas_call x1, Pallas kernels, local(): pl.pallas_call(first_kernel, out_shape=f32(ROWS, COLS), in_specs=[VMEM] *...  1.11 us
    pallas_call x1, Pallas kernels, local(): pl.pallas_call(last_kernel, out_shape=f32(ROWS, COLS), in_specs=[HBM, VME...  1.11 us
    unnamed x20, local copies, waits for them, and re-layouts  1.06 us
  transfers between devices with their start and end apart: 6, of which 3 were waited for; matrix products, arithmetic and copies ran while one was open for 2% of the time, Pallas kernels for 5%

profile of v3, /device:TPU:1, one launch (start us, length us, event | category | flops | bytes accessed | tf_op | source)
XLA Modules:
  0.0 42.0 jit_solution(17363877578128890998)
XLA Ops:
  0.0 0.0 copy-start.6
  0.0 3.2 %collective-permute-start.2 = (f32[1760,128]{1,0:T(8,128)}, f32[1760,128]{1,0:T(8,128)S(1)}, u32[]{:S(2)}, u32[]{:S(2)}) collective-permute-start(f32[1760,128]{1,0:T(8,128)} %bitcast.10), channel_id=1, source_target_pairs={{0,128},{128,0},{1,129},{129,1},{2,130},{130,2},{3,131},{131,3},{4... | collective-permute-start | bytes 2703368 | tf_op jit(solution)/shard_map/ppermute | solution.py:421
  3.2 0.7 %convert_element_type.6 = f32[2,500]{1,0:T(2,128)S(1)} convert(s32[2,500]{1,0:T(2,128)} %param.19) | non-fusion elementwise | flops 1000 | bytes 8000 | tf_op jit(solution)/shard_map/convert_element_type | solution.py:425
  3.9 0.0 copy-done.6
  3.9 0.0 copy-start.7
  3.9 0.0 copy-start.9
  4.0 0.0 copy-start.8
  4.0 0.7 %copy-done.7 = f32[2,500]{1,0:T(2,128)S(1)} copy-done((f32[2,500]{1,0:T(2,128)S(1)}, f32[2,500]{1,0:T(2,128)}, u32[]{:S(2)}) %copy-start.7) | copy-done | bytes 4024
  4.6 0.0 copy-done.9
  4.6 0.0 copy-done.8
  4.7 0.0 copy-start
  4.7 0.0 copy-start.1
  4.7 0.0 copy-start.2
  4.7 0.0 copy-start.4
  4.7 0.4 prepare.1
  5.1 0.0 copy-start.3
  5.1 0.4 collective-permute-done.2.swapped
  5.5 0.3 copy-done
  5.9 0.0 copy-done.1
  5.9 0.0 copy-done.2
  5.9 0.0 copy-done.4
  5.9 0.0 copy-done.3
  5.9 6.2 %chemistry.1 = (f32[896,128]{1,0:T(8,128)}, f32[896,128]{1,0:T(8,128)S(1)}) custom-call(f32[1760,128]{1,0:T(8,128)S(1)} %bitcast.11, f32[1760,128]{1,0:T(8,128)S(1)} %collective-permute-done.2.swapped, s32[128,128]{1,0:T(8,128)S(1)} %bitcast.14, s32[128,128]{1,0:T(8,128)S(1)} %bitcast.15, f32[8,128]{1,0:T(8,128)S(1)} %copy-done.3, f32[8,128]{1,0:T(8,128)S(1)} %copy-done.4, ...), custom_call_target="tpu_custom_call" | custom-call | flops 6000000000 | bytes 12000000 | tf_op jit(solution)/shard_map/chemistry/pallas_call | solution.py:442
  12.1 0.0 copy-start.5
  12.1 16.6 %all-to-all-start = ((f32[128,1,896]{2,1,0:T(1,128)}), f32[128,1,896]{2,1,0:T(1,128)S(1)}, u32[]{:S(2)}, u32[]{:S(2)}) async-start(f32[128,1,896]{2,1,0:T(1,128)} %bitcast.5), calls=%async_computation | async-start | bytes 917504 | tf_op jit(solution)/shard_map/all_to_all | solution.py:469
  28.8 0.7 %collective-permute-start.3 = (f32[896,128]{1,0:T(8,128)S(1)}, f32[896,128]{1,0:T(8,128)S(1)}, u32[]{:S(2)}, u32[]{:S(2)}) collective-permute-start(f32[896,128]{1,0:T(8,128)S(1)} %get-tuple-element.17.own_tend), channel_id=1, source_target_pairs={{0,128},{128,0},{1,129},{129,1},{2,130},{130,2},{3,131},{131,3},{4... | collective-permute-start | bytes 1376264 | tf_op jit(solution)/shard_map/ppermute | solution.py:492
  29.5 0.0 copy-done.5
  29.5 0.4 edges.1
  29.9 0.7 %collective-permute-start = (f32[32,256]{1,0:T(8,128)S(1)}, f32[32,256]{1,0:T(8,128)S(1)}, u32[]{:S(2)}, u32[]{:S(2)}) collective-permute-start(f32[32,256]{1,0:T(8,128)S(1)} %get-tuple-element.13), channel_id=1, source_target_pairs={{1,2},{2,1},{3,4},{4,3},{5,6},{6,5},{7,8},{8,7},{9,10},{10,9},{11,... | collective-permute-start | bytes 98312 | tf_op jit(solution)/shard_map/ppermute | solution.py:490
  30.6 0.7 %collective-permute-start.1 = (f32[32,256]{1,0:T(8,128)S(1)}, f32[32,256]{1,0:T(8,128)S(1)}, u32[]{:S(2)}, u32[]{:S(2)}) collective-permute-start(f32[32,256]{1,0:T(8,128)S(1)} %get-tuple-element.14), channel_id=1, source_target_pairs={{0,1},{1,0},{2,3},{3,2},{4,5},{5,4},{6,7},{7,6},{8,9},{9,8},{10,11... | collective-permute-start | bytes 98312 | tf_op jit(solution)/shard_map/ppermute | solution.py:491
  31.2 0.0 collective-permute-done.3.other_tend
  31.2 6.7 %all-to-all-done = f32[128,1,896]{2,1,0:T(1,128)S(1)} async-done(((f32[128,1,896]{2,1,0:T(1,128)}), f32[128,1,896]{2,1,0:T(1,128)S(1)}, u32[]{:S(2)}, u32[]{:S(2)}) %all-to-all-start) | async-done | bytes 458784 | tf_op jit(solution)/shard_map/all_to_all | solution.py:469
  38.0 1.5 %collective-permute-start.4 = (f32[896,128]{1,0:T(8,128)S(1)}, f32[896,128]{1,0:T(8,128)S(1)}, u32[]{:S(2)}, u32[]{:S(2)}) collective-permute-start(f32[896,128]{1,0:T(8,128)S(1)} %bitcast.8), channel_id=1, source_target_pairs={{0,128},{128,0},{1,129},{129,1},{2,130},{130,2},{3,131},{131,3},{4... | collective-permute-start | bytes 1376264 | tf_op jit(solution)/shard_map/ppermute | solution.py:495
  39.4 0.0 collective-permute-done.far
  39.4 0.0 collective-permute-done.1.near
  39.5 1.1 %first.1.base = f32[1760,128]{1,0:T(8,128)} custom-call(f32[1760,128]{1,0:T(8,128)S(1)} %bitcast.13, f32[8,128]{1,0:T(8,128)S(1)} %copy-done.5, f32[32,256]{1,0:T(8,128)S(1)} %collective-permute-done.far, f32[32,256]{1,0:T(8,128)S(1)} %collective-permute-done.1.near, f32[896,128]{1,0:T(8,128)S(1)} %get-tuple-element.17.own_tend, ...), custom_call_target="tpu_custom_call" | custom-call | flops 20000000000 | bytes 40000000 | tf_op jit(solution)/shard_map/first/pallas_call | solution.py:496
  40.6 0.3 collective-permute-done.4.other
  40.9 1.1 %last.1 = f32[1760,128]{1,0:T(8,128)} custom-call(f32[1760,128]{1,0:T(8,128)} %first.1.base, f32[896,128]{1,0:T(8,128)S(1)} %collective-permute-done.4.other), custom_call_target="tpu_custom_call", output_to_operand_aliasing={{}: (0, {})} | custom-call | flops 1000000000 | bytes 2000000 | tf_op jit(solution)/shard_map/last/pallas_call | solution.py:518
  (2 shorter events, 0.0 us)
Async XLA Ops:
  0.0 3.9 %copy-start.6 = (s32[2,500]{1,0:T(2,128)S(1)}, s32[2,500]{1,0:T(2,128)}, u32[]{:S(2)}) copy-start(s32[2,500]{1,0:T(2,128)} %param.20) | copy-start | bytes 12004
  0.0 5.5 %collective-permute-start.2 = (f32[1760,128]{1,0:T(8,128)}, f32[1760,128]{1,0:T(8,128)S(1)}, u32[]{:S(2)}, u32[]{:S(2)}) collective-permute-start(f32[1760,128]{1,0:T(8,128)} %bitcast.10), channel_id=1, source_target_pairs={{0,128},{128,0},{1,129},{129,1},{2,130},{130,2},{3,131},{131,3},{4... | collective-permute-start | bytes 2703368 | tf_op jit(solution)/shard_map/ppermute | solution.py:421
  3.9 0.7 %copy-start.7 = (f32[2,500]{1,0:T(2,128)S(1)}, f32[2,500]{1,0:T(2,128)}, u32[]{:S(2)}) copy-start(f32[2,500]{1,0:T(2,128)} %param.21) | copy-start | bytes 12004
  3.9 0.7 %copy-start.9 = (f32[500]{0:T(512)S(1)}, f32[500]{0:T(512)}, u32[]{:S(2)}) copy-start(f32[500]{0:T(512)} %param.18) | copy-start | bytes 6004
  4.0 0.7 %copy-start.8 = (f32[500]{0:T(512)S(1)}, f32[500]{0:T(512)}, u32[]{:S(2)}) copy-start(f32[500]{0:T(512)} %param.17) | copy-start | bytes 6004
  4.7 1.2 %copy-start = (f32[1,220,8,128]{3,2,1,0:T(8,128)S(1)}, f32[1,220,8,128]{3,2,1,0:T(8,128)}, u32[]{:S(2)}) copy-start(f32[1,220,8,128]{3,2,1,0:T(8,128)} %param.11) | copy-start | bytes 2703364
  4.7 1.2 %copy-start.1 = (s32[16384]{0:T(1024)S(1)}, s32[16384]{0:T(1024)}, u32[]{:S(2)}) copy-start(s32[16384]{0:T(1024)} %param.15) | copy-start | bytes 196612
  4.7 1.2 %copy-start.2 = (s32[16384]{0:T(1024)S(1)}, s32[16384]{0:T(1024)}, u32[]{:S(2)}) copy-start(s32[16384]{0:T(1024)} %param.16) | copy-start | bytes 196612
  4.7 1.1 %copy-start.4 = (f32[8,128]{1,0:T(8,128)S(1)}, f32[8,128]{1,0:T(8,128)}, u32[]{:S(2)}) copy-start(f32[8,128]{1,0:T(8,128)} %light.1) | copy-start | bytes 12292
  5.1 0.8 %copy-start.3 = (f32[8,128]{1,0:T(8,128)S(1)}, f32[8,128]{1,0:T(8,128)}, u32[]{:S(2)}) copy-start(f32[8,128]{1,0:T(8,128)} %heat.1) | copy-start | bytes 12292
  12.1 17.4 %copy-start.5 = (f32[8,128]{1,0:T(8,128)S(1)}, f32[8,128]{1,0:T(8,128)}, u32[]{:S(2)}) copy-start(f32[8,128]{1,0:T(8,128)} %wind.3) | copy-start | bytes 12292
  12.1 25.8 %all-to-all-start = ((f32[128,1,896]{2,1,0:T(1,128)}), f32[128,1,896]{2,1,0:T(1,128)S(1)}, u32[]{:S(2)}, u32[]{:S(2)}) async-start(f32[128,1,896]{2,1,0:T(1,128)} %bitcast.5), calls=%async_computation | async-start | bytes 917504 | tf_op jit(solution)/shard_map/all_to_all | solution.py:469
  28.8 2.5 %collective-permute-start.3 = (f32[896,128]{1,0:T(8,128)S(1)}, f32[896,128]{1,0:T(8,128)S(1)}, u32[]{:S(2)}, u32[]{:S(2)}) collective-permute-start(f32[896,128]{1,0:T(8,128)S(1)} %get-tuple-element.17.own_tend), channel_id=1, source_target_pairs={{0,128},{128,0},{1,129},{129,1},{2,130},{130,2},{3,131},{131,3},{4... | collective-permute-start | bytes 1376264 | tf_op jit(solution)/shard_map/ppermute | solution.py:492
  29.9 9.6 %collective-permute-start = (f32[32,256]{1,0:T(8,128)S(1)}, f32[32,256]{1,0:T(8,128)S(1)}, u32[]{:S(2)}, u32[]{:S(2)}) collective-permute-start(f32[32,256]{1,0:T(8,128)S(1)} %get-tuple-element.13), channel_id=1, source_target_pairs={{1,2},{2,1},{3,4},{4,3},{5,6},{6,5},{7,8},{8,7},{9,10},{10,9},{11,... | collective-permute-start | bytes 98312 | tf_op jit(solution)/shard_map/ppermute | solution.py:490
  30.6 8.9 %collective-permute-start.1 = (f32[32,256]{1,0:T(8,128)S(1)}, f32[32,256]{1,0:T(8,128)S(1)}, u32[]{:S(2)}, u32[]{:S(2)}) collective-permute-start(f32[32,256]{1,0:T(8,128)S(1)} %get-tuple-element.14), channel_id=1, source_target_pairs={{0,1},{1,0},{2,3},{3,2},{4,5},{5,4},{6,7},{7,6},{8,9},{9,8},{10,11... | collective-permute-start | bytes 98312 | tf_op jit(solution)/shard_map/ppermute | solution.py:491
  38.0 2.9 %collective-permute-start.4 = (f32[896,128]{1,0:T(8,128)S(1)}, f32[896,128]{1,0:T(8,128)S(1)}, u32[]{:S(2)}, u32[]{:S(2)}) collective-permute-start(f32[896,128]{1,0:T(8,128)S(1)} %bitcast.8), channel_id=1, source_target_pairs={{0,128},{128,0},{1,129},{129,1},{2,130},{130,2},{3,131},{131,3},{4... | collective-permute-start | bytes 1376264 | tf_op jit(solution)/shard_map/ppermute | solution.py:495

commit v4 on v3

--- a/solution.py
+++ b/solution.py
@@ -103,11 +103,20 @@
     gather[...] = jnp.transpose(turning[...]).astype(jnp.bfloat16)
 
 
+def choose_kernel(lookup, choose):
+    tile = lax.axis_index("tile")
+    lane = lax.broadcasted_iota(jnp.int32, (COLS, COLS), 1)
+    column = jnp.sum(jnp.where(lane == tile, lookup[...], 0), axis=1, keepdims=True)
+    chosen = jnp.where(lane == column - tile * COLS, 1.0, 0.0)
+    ordered = jnp.where(lane == tile_at(lax.broadcasted_iota(jnp.int32, (COLS, COLS), 0)), 1.0, 0.0)
+    choose[...] = dot(ordered.astype(jnp.bfloat16), chosen.astype(jnp.bfloat16)).astype(jnp.bfloat16)
+
+
 def chemistry_kernel(
     own,
     swapped,
     marker,
-    lookup,
+    choose,
     heat,
     light,
     weights,
@@ -170,11 +179,6 @@
         sweep()
         sweep()
 
-    lane = lax.broadcasted_iota(jnp.int32, (COLS, COLS), 1)
-    column = jnp.sum(jnp.where(lane == tile, lookup[...], 0), axis=1, keepdims=True)
-    chosen = jnp.where(lane == column - tile * COLS, 1.0, 0.0)
-    ordered = jnp.where(lane == tile_at(lax.broadcasted_iota(jnp.int32, (COLS, COLS), 0)), 1.0, 0.0)
-    choose = dot(ordered.astype(jnp.bfloat16), chosen.astype(jnp.bfloat16)).astype(jnp.bfloat16)
     for layer in range(HALF):
         cells = pl.ds(layer * COLS, COLS)
         stack[pl.ds(layer, SPEC, stride=HALF), :] = now[0:SPEC, cells]
@@ -189,7 +193,7 @@
     owners = COLS // SENDS
     for part in range(SENDS):
         turned = dot(
-            jnp.concatenate([choose[part * owners : (part + 1) * owners]] * PARTS, axis=1),
+            jnp.concatenate([choose[part * owners : (part + 1) * owners, :]] * PARTS, axis=1),
             parts[...],
         )
         for piece in range(PIECES):
@@ -439,6 +443,15 @@
         cost_estimate=cost(1),
         name="prepare",
     )(table)
+    choose = pl.pallas_call(
+        choose_kernel,
+        out_shape=bf16(COLS, COLS),
+        in_specs=[VMEM],
+        out_specs=VMEM,
+        compiler_params=PARAMS,
+        cost_estimate=cost(1),
+        name="choose",
+    )(position_vertical_lookup.reshape(COLS, COLS))
     send, tendency = pl.pallas_call(
         chemistry_kernel,
         out_shape=(f32(PACKED, COLS), f32(HALF * SPAD, COLS)),
@@ -460,7 +473,7 @@
             amounts,
         swapped,
         illuminated_marker.reshape(COLS, COLS),
-        position_vertical_lookup.reshape(COLS, COLS),
+        choose,
         air_warmth_kelvin,
         sunlight_strength,
         weights,

time: 41.4 us -> 42.9 us (1.036); the launches traced: 42 us -> 42.7 us
  local copies, waits for them, and re-layouts: 1.09 us -> 2.09 us
    unnamed x20, local copies, waits for them, and re-layouts: 1.06 us -> 2.06 us
  transfers between devices with their start and end apart: 6 -> 6, of which waited for: 3 -> 2; matrix products, arithmetic and copies ran while one was open for 2% -> 2% of each run, Pallas kernels for 5% -> 5%
where the time goes in v4:
time: 42.9 us; the launch traced here: 42.7 us
  starting transfers between devices  23.4 us (55%)
  Pallas kernels  9.38 us (22%)
  waiting for transfers between devices  7.07 us (16%)
  local copies, waits for them, and re-layouts  2.09 us (5%)
  other arithmetic  0.69 us (2%)
    all_to_all x1, starting transfers between devices, local(): lax.all_to_all(send.reshape(COLS, 1, PACKED), 'tile', split_axis=0, conca...  16.6 us
    all_to_all x1, waiting for transfers between devices, local(): lax.all_to_all(send.reshape(COLS, 1, PACKED), 'tile', split_axis=0, conca...  6.74 us
    pallas_call x1, Pallas kernels, local(): pl.pallas_call(chemistry_kernel, out_shape=(f32(PACKED, COLS), f32(HALF *...  6.12 us
    ppermute x1, starting transfers between devices, local(): swapped = lax.ppermute(amounts, 'group', swap)  3.24 us
    unnamed x20, local copies, waits for them, and re-layouts  2.06 us
    ppermute x1, starting transfers between devices, local(): other_received = lax.ppermute(received, 'group', swap)  1.53 us
    pallas_call x1, Pallas kernels, local(): pl.pallas_call(first_kernel, out_shape=f32(ROWS, COLS), in_specs=[VMEM] *...  1.11 us
    pallas_call x1, Pallas kernels, local(): pl.pallas_call(last_kernel, out_shape=f32(ROWS, COLS), in_specs=[HBM, VME...  1.11 us
  transfers between devices with their start and end apart: 6, of which 2 were waited for; matrix products, arithmetic and copies ran while one was open for 2% of the time, Pallas kernels for 5%

profile of v4, /device:TPU:1, one launch (start us, length us, event | category | flops | bytes accessed | tf_op | source)
XLA Modules:
  0.0 42.7 jit_solution(4238693987754758988)
XLA Ops:
  0.0 0.0 copy-start.6
  0.0 3.2 %collective-permute-start.2 = (f32[1760,128]{1,0:T(8,128)}, f32[1760,128]{1,0:T(8,128)S(1)}, u32[]{:S(2)}, u32[]{:S(2)}) collective-permute-start(f32[1760,128]{1,0:T(8,128)} %bitcast.10), channel_id=1, source_target_pairs={{0,128},{128,0},{1,129},{129,1},{2,130},{130,2},{3,131},{131,3},{4... | collective-permute-start | bytes 2703368 | tf_op jit(solution)/shard_map/ppermute | solution.py:425
  3.2 0.7 %convert_element_type.6 = f32[2,500]{1,0:T(2,128)S(1)} convert(s32[2,500]{1,0:T(2,128)} %param.19) | non-fusion elementwise | flops 1000 | bytes 8000 | tf_op jit(solution)/shard_map/convert_element_type | solution.py:429
  3.9 0.0 copy-done.6
  3.9 0.0 copy-start.7
  3.9 0.0 copy-start.9
  4.0 0.0 copy-start.8
  4.0 0.7 %copy-done.7 = f32[2,500]{1,0:T(2,128)S(1)} copy-done((f32[2,500]{1,0:T(2,128)S(1)}, f32[2,500]{1,0:T(2,128)}, u32[]{:S(2)}) %copy-start.7) | copy-done | bytes 4024
  4.6 0.0 copy-done.9
  4.6 0.0 copy-done.8
  4.7 0.0 copy-start.1
  4.7 0.4 prepare.1
  5.1 0.4 %copy-done.1 = s32[16384]{0:T(1024)S(1)} copy-done((s32[16384]{0:T(1024)S(1)}, s32[16384]{0:T(1024)}, u32[]{:S(2)}) %copy-start.1) | copy-done | bytes 65560
  5.5 0.0 copy-start
  5.5 0.0 copy-start.2
  5.5 0.0 copy-start.4
  5.5 0.2 choose.1
  5.8 0.0 copy-start.3
  5.8 0.0 collective-permute-done.2.swapped
  5.8 0.9 %copy-done = f32[1,220,8,128]{3,2,1,0:T(8,128)S(1)} copy-done((f32[1,220,8,128]{3,2,1,0:T(8,128)S(1)}, f32[1,220,8,128]{3,2,1,0:T(8,128)}, u32[]{:S(2)}) %copy-start) | copy-done | bytes 901144
  6.7 0.0 copy-done.2
  6.7 0.0 copy-done.4
  6.7 0.0 copy-done.3
  6.7 6.1 %chemistry.1 = (f32[896,128]{1,0:T(8,128)}, f32[896,128]{1,0:T(8,128)S(1)}) custom-call(f32[1760,128]{1,0:T(8,128)S(1)} %bitcast.11, f32[1760,128]{1,0:T(8,128)S(1)} %collective-permute-done.2.swapped, s32[128,128]{1,0:T(8,128)S(1)} %bitcast.15, bf16[128,128]{1,0:T(8,128)(2,1)S(1)} %choose.1, f32[8,128]{1,0:T(8,128)S(1)} %copy-done.3, ...), custom_call_target="tpu_custom_call" | custom-call | flops 6000000000 | bytes 12000000 | tf_op jit(solution)/shard_map/chemistry/pallas_call | solution.py:455
  12.8 0.0 copy-start.5
  12.8 16.6 %all-to-all-start = ((f32[128,1,896]{2,1,0:T(1,128)}), f32[128,1,896]{2,1,0:T(1,128)S(1)}, u32[]{:S(2)}, u32[]{:S(2)}) async-start(f32[128,1,896]{2,1,0:T(1,128)} %bitcast.5), calls=%async_computation | async-start | bytes 917504 | tf_op jit(solution)/shard_map/all_to_all | solution.py:482
  29.5 0.6 %collective-permute-start.3 = (f32[896,128]{1,0:T(8,128)S(1)}, f32[896,128]{1,0:T(8,128)S(1)}, u32[]{:S(2)}, u32[]{:S(2)}) collective-permute-start(f32[896,128]{1,0:T(8,128)S(1)} %get-tuple-element.17.own_tend), channel_id=1, source_target_pairs={{0,128},{128,0},{1,129},{129,1},{2,130},{130,2},{3,131},{131,3},{4... | collective-permute-start | bytes 1376264 | tf_op jit(solution)/shard_map/ppermute | solution.py:505
  30.1 0.0 copy-done.5
  30.1 0.4 edges.1
  30.5 0.7 %collective-permute-start = (f32[32,256]{1,0:T(8,128)S(1)}, f32[32,256]{1,0:T(8,128)S(1)}, u32[]{:S(2)}, u32[]{:S(2)}) collective-permute-start(f32[32,256]{1,0:T(8,128)S(1)} %get-tuple-element.13), channel_id=1, source_target_pairs={{1,2},{2,1},{3,4},{4,3},{5,6},{6,5},{7,8},{8,7},{9,10},{10,9},{11,... | collective-permute-start | bytes 98312 | tf_op jit(solution)/shard_map/ppermute | solution.py:503
  31.2 0.7 %collective-permute-start.1 = (f32[32,256]{1,0:T(8,128)S(1)}, f32[32,256]{1,0:T(8,128)S(1)}, u32[]{:S(2)}, u32[]{:S(2)}) collective-permute-start(f32[32,256]{1,0:T(8,128)S(1)} %get-tuple-element.14), channel_id=1, source_target_pairs={{0,1},{1,0},{2,3},{3,2},{4,5},{5,4},{6,7},{7,6},{8,9},{9,8},{10,11... | collective-permute-start | bytes 98312 | tf_op jit(solution)/shard_map/ppermute | solution.py:504
  31.9 0.0 collective-permute-done.3.other_tend
  31.9 6.7 %all-to-all-done = f32[128,1,896]{2,1,0:T(1,128)S(1)} async-done(((f32[128,1,896]{2,1,0:T(1,128)}), f32[128,1,896]{2,1,0:T(1,128)S(1)}, u32[]{:S(2)}, u32[]{:S(2)}) %all-to-all-start) | async-done | bytes 458784 | tf_op jit(solution)/shard_map/all_to_all | solution.py:482
  38.6 1.5 %collective-permute-start.4 = (f32[896,128]{1,0:T(8,128)S(1)}, f32[896,128]{1,0:T(8,128)S(1)}, u32[]{:S(2)}, u32[]{:S(2)}) collective-permute-start(f32[896,128]{1,0:T(8,128)S(1)} %bitcast.8), channel_id=1, source_target_pairs={{0,128},{128,0},{1,129},{129,1},{2,130},{130,2},{3,131},{131,3},{4... | collective-permute-start | bytes 1376264 | tf_op jit(solution)/shard_map/ppermute | solution.py:508
  40.2 0.0 collective-permute-done.far
  40.2 0.0 collective-permute-done.1.near
  40.2 1.1 %first.1.base = f32[1760,128]{1,0:T(8,128)} custom-call(f32[1760,128]{1,0:T(8,128)S(1)} %bitcast.13, f32[8,128]{1,0:T(8,128)S(1)} %copy-done.5, f32[32,256]{1,0:T(8,128)S(1)} %collective-permute-done.far, f32[32,256]{1,0:T(8,128)S(1)} %collective-permute-done.1.near, f32[896,128]{1,0:T(8,128)S(1)} %get-tuple-element.17.own_tend, ...), custom_call_target="tpu_custom_call" | custom-call | flops 20000000000 | bytes 40000000 | tf_op jit(solution)/shard_map/first/pallas_call | solution.py:509
  41.3 0.3 collective-permute-done.4.other
  41.6 1.1 %last.1 = f32[1760,128]{1,0:T(8,128)} custom-call(f32[1760,128]{1,0:T(8,128)} %first.1.base, f32[896,128]{1,0:T(8,128)S(1)} %collective-permute-done.4.other), custom_call_target="tpu_custom_call", output_to_operand_aliasing={{}: (0, {})} | custom-call | flops 1000000000 | bytes 2000000 | tf_op jit(solution)/shard_map/last/pallas_call | solution.py:531
  (2 shorter events, 0.0 us)
Async XLA Ops:
  0.0 3.9 %copy-start.6 = (s32[2,500]{1,0:T(2,128)S(1)}, s32[2,500]{1,0:T(2,128)}, u32[]{:S(2)}) copy-start(s32[2,500]{1,0:T(2,128)} %param.20) | copy-start | bytes 12004
  0.0 5.8 %collective-permute-start.2 = (f32[1760,128]{1,0:T(8,128)}, f32[1760,128]{1,0:T(8,128)S(1)}, u32[]{:S(2)}, u32[]{:S(2)}) collective-permute-start(f32[1760,128]{1,0:T(8,128)} %bitcast.10), channel_id=1, source_target_pairs={{0,128},{128,0},{1,129},{129,1},{2,130},{130,2},{3,131},{131,3},{4... | collective-permute-start | bytes 2703368 | tf_op jit(solution)/shard_map/ppermute | solution.py:425
  3.9 0.7 %copy-start.7 = (f32[2,500]{1,0:T(2,128)S(1)}, f32[2,500]{1,0:T(2,128)}, u32[]{:S(2)}) copy-start(f32[2,500]{1,0:T(2,128)} %param.21) | copy-start | bytes 12004
  3.9 0.7 %copy-start.9 = (f32[500]{0:T(512)S(1)}, f32[500]{0:T(512)}, u32[]{:S(2)}) copy-start(f32[500]{0:T(512)} %param.18) | copy-start | bytes 6004
  4.0 0.7 %copy-start.8 = (f32[500]{0:T(512)S(1)}, f32[500]{0:T(512)}, u32[]{:S(2)}) copy-start(f32[500]{0:T(512)} %param.17) | copy-start | bytes 6004
  4.7 0.8 %copy-start.1 = (s32[16384]{0:T(1024)S(1)}, s32[16384]{0:T(1024)}, u32[]{:S(2)}) copy-start(s32[16384]{0:T(1024)} %param.16) | copy-start | bytes 196612
  5.5 1.2 %copy-start = (f32[1,220,8,128]{3,2,1,0:T(8,128)S(1)}, f32[1,220,8,128]{3,2,1,0:T(8,128)}, u32[]{:S(2)}) copy-start(f32[1,220,8,128]{3,2,1,0:T(8,128)} %param.11) | copy-start | bytes 2703364
  5.5 1.2 %copy-start.2 = (s32[16384]{0:T(1024)S(1)}, s32[16384]{0:T(1024)}, u32[]{:S(2)}) copy-start(s32[16384]{0:T(1024)} %param.15) | copy-start | bytes 196612
  5.5 1.2 %copy-start.4 = (f32[8,128]{1,0:T(8,128)S(1)}, f32[8,128]{1,0:T(8,128)}, u32[]{:S(2)}) copy-start(f32[8,128]{1,0:T(8,128)} %light.1) | copy-start | bytes 12292
  5.8 0.9 %copy-start.3 = (f32[8,128]{1,0:T(8,128)S(1)}, f32[8,128]{1,0:T(8,128)}, u32[]{:S(2)}) copy-start(f32[8,128]{1,0:T(8,128)} %heat.1) | copy-start | bytes 12292
  12.8 17.3 %copy-start.5 = (f32[8,128]{1,0:T(8,128)S(1)}, f32[8,128]{1,0:T(8,128)}, u32[]{:S(2)}) copy-start(f32[8,128]{1,0:T(8,128)} %wind.3) | copy-start | bytes 12292
  12.8 25.8 %all-to-all-start = ((f32[128,1,896]{2,1,0:T(1,128)}), f32[128,1,896]{2,1,0:T(1,128)S(1)}, u32[]{:S(2)}, u32[]{:S(2)}) async-start(f32[128,1,896]{2,1,0:T(1,128)} %bitcast.5), calls=%async_computation | async-start | bytes 917504 | tf_op jit(solution)/shard_map/all_to_all | solution.py:482
  29.5 2.4 %collective-permute-start.3 = (f32[896,128]{1,0:T(8,128)S(1)}, f32[896,128]{1,0:T(8,128)S(1)}, u32[]{:S(2)}, u32[]{:S(2)}) collective-permute-start(f32[896,128]{1,0:T(8,128)S(1)} %get-tuple-element.17.own_tend), channel_id=1, source_target_pairs={{0,128},{128,0},{1,129},{129,1},{2,130},{130,2},{3,131},{131,3},{4... | collective-permute-start | bytes 1376264 | tf_op jit(solution)/shard_map/ppermute | solution.py:505
  30.5 9.6 %collective-permute-start = (f32[32,256]{1,0:T(8,128)S(1)}, f32[32,256]{1,0:T(8,128)S(1)}, u32[]{:S(2)}, u32[]{:S(2)}) collective-permute-start(f32[32,256]{1,0:T(8,128)S(1)} %get-tuple-element.13), channel_id=1, source_target_pairs={{1,2},{2,1},{3,4},{4,3},{5,6},{6,5},{7,8},{8,7},{9,10},{10,9},{11,... | collective-permute-start | bytes 98312 | tf_op jit(solution)/shard_map/ppermute | solution.py:503
  31.2 9.0 %collective-permute-start.1 = (f32[32,256]{1,0:T(8,128)S(1)}, f32[32,256]{1,0:T(8,128)S(1)}, u32[]{:S(2)}, u32[]{:S(2)}) collective-permute-start(f32[32,256]{1,0:T(8,128)S(1)} %get-tuple-element.14), channel_id=1, source_target_pairs={{0,1},{1,0},{2,3},{3,2},{4,5},{5,4},{6,7},{7,6},{8,9},{9,8},{10,11... | collective-permute-start | bytes 98312 | tf_op jit(solution)/shard_map/ppermute | solution.py:504
  38.6 3.0 %collective-permute-start.4 = (f32[896,128]{1,0:T(8,128)S(1)}, f32[896,128]{1,0:T(8,128)S(1)}, u32[]{:S(2)}, u32[]{:S(2)}) collective-permute-start(f32[896,128]{1,0:T(8,128)S(1)} %bitcast.8), channel_id=1, source_target_pairs={{0,128},{128,0},{1,129},{129,1},{2,130},{130,2},{3,131},{131,3},{4... | collective-permute-start | bytes 1376264 | tf_op jit(solution)/shard_map/ppermute | solution.py:508
